TPU v7x, 512 devices: a whole 4x8x8 slice. The times are simulated.
512 devices in a mesh: dp: 32 (over y, x), ctx: 16 (over z, core).
Axes of the slice: x: 4, y: 8, z: 8, core: 2. Of those that a mesh axis runs over, the one named last changes fastest.
Arguments:
- queries: bfloat16 [32, 2048, 4096], P('dp', 'ctx'), may hold values from -8 to 8
- keys: bfloat16 [32, 2048, 1024], P('dp', 'ctx'), may hold values from -8 to 8
- values: bfloat16 [32, 2048, 1024], P('dp', 'ctx'), may hold values from -6 to 6
- grad_out: bfloat16 [32, 2048, 4096], P('dp', 'ctx'), may hold values from -16 to 16
- sink_logit: float32 [32], P('ctx'), may hold values from 1 to 4
- doc_lengths: int32 [32, 16], P('dp'), may hold values from 1 to 256, 2048 in all within a row
- slab_order: int32 [32, 32], P('dp'), may hold values from 0 to 31, each once within a row
Outputs:
- grad_queries: bfloat16 [32, 2048, 4096], P('dp', 'ctx')
- grad_keys: bfloat16 [32, 2048, 1024], P('dp', 'ctx')
- grad_values: bfloat16 [32, 2048, 1024], P('dp', 'ctx')
- grad_sink: float32 [32], P('ctx')
Inputs may be any that keep to these rules, and one draw needn't show every extreme that they name: `doc_lengths`: the longest document has exactly 256 tokens. `slab_order`: each row is a permutation of the slabs.
All inputs are finite; a program needn't handle non-finite values.
Results may differ from a plain program's by a relative error of at most 0.02.
Values may be sent and summed in bfloat16 or wider, within the bound.
A program may use at most 64 MiB of HBM per device.

v0:
```python
import math

import jax
import jax.numpy as jnp
from jax import lax
from jax.sharding import PartitionSpec as P

HD = 128


masked_score = -1e30


def doc_index(lengths, positions):
    doc_ends = jnp.cumsum(lengths)
    return jnp.sum((positions[:, None] >= doc_ends[None, :]).astype(jnp.int32), axis=1)


def head_group(query_all, key_all, value_all, grad_all, sinks, lengths):
    seq_len, head_count, head_width = query_all.shape
    block_rows = min(512, seq_len)
    reach_rows = min(256, seq_len // 4)
    span_rows = block_rows + reach_rows
    factor = 1.0 / math.sqrt(head_width)
    doc_ids = doc_index(lengths, jnp.arange(seq_len, dtype=jnp.int32))
    pad_keys = jnp.concatenate([jnp.zeros((reach_rows, head_width), key_all.dtype), key_all], 0)
    pad_values = jnp.concatenate(
        [jnp.zeros((reach_rows, head_width), value_all.dtype), value_all], 0
    )
    pad_docs = jnp.concatenate([jnp.full((reach_rows,), -1, jnp.int32), doc_ids], 0)

    def one_block(totals, block_index):
        key_total, value_total = totals
        first_row = block_index * block_rows
        query_rows = lax.dynamic_slice_in_dim(query_all, first_row, block_rows, 0)
        grad_rows = lax.dynamic_slice_in_dim(grad_all, first_row, block_rows, 0)
        key_rows = lax.dynamic_slice_in_dim(pad_keys, first_row, span_rows, 0)
        value_rows = lax.dynamic_slice_in_dim(pad_values, first_row, span_rows, 0)
        query_doc = lax.dynamic_slice_in_dim(doc_ids, first_row, block_rows, 0)
        key_doc = lax.dynamic_slice_in_dim(pad_docs, first_row, span_rows, 0)
        query_place = first_row + jnp.arange(block_rows, dtype=jnp.int32)
        key_place = first_row - reach_rows + jnp.arange(span_rows, dtype=jnp.int32)
        allowed = (query_doc[:, None] == key_doc[None, :]) & (
            key_place[None, :] <= query_place[:, None]
        )
        scores = (
            jnp.einsum("bhd,kd->hbk", query_rows, key_rows, preferred_element_type=jnp.float32)
            * factor
        )
        scores = jnp.where(allowed[None], scores, masked_score)
        maxima = jnp.maximum(sinks[:, None], jnp.max(scores, axis=2))
        weights = jnp.exp(scores - maxima[:, :, None])
        sink_weight = jnp.exp(sinks[:, None] - maxima)
        row_total = sink_weight + jnp.sum(weights, axis=2)
        softmax = weights / row_total[:, :, None]
        sink_share = sink_weight / row_total
        rounded = softmax.astype(jnp.bfloat16)
        attended = jnp.einsum(
            "hbk,kd->bhd", rounded, value_rows, preferred_element_type=jnp.float32
        ).astype(jnp.bfloat16)
        row_delta = jnp.sum(grad_rows.astype(jnp.float32) * attended.astype(jnp.float32), axis=2).T
        grad_prob = jnp.einsum(
            "bhd,kd->hbk", grad_rows, value_rows, preferred_element_type=jnp.float32
        )
        grad_score = (softmax * (grad_prob - row_delta[:, :, None])).astype(jnp.bfloat16)
        query_grad = (
            jnp.einsum("hbk,kd->bhd", grad_score, key_rows, preferred_element_type=jnp.float32)
            * factor
        ).astype(jnp.bfloat16)
        key_grad = (
            jnp.einsum("hbk,bhd->kd", grad_score, query_rows, preferred_element_type=jnp.float32)
            * factor
        )
        value_grad = jnp.einsum(
            "hbk,bhd->kd", rounded, grad_rows, preferred_element_type=jnp.float32
        )
        key_total = lax.dynamic_update_slice_in_dim(
            key_total,
            lax.dynamic_slice_in_dim(key_total, first_row, span_rows, 0) + key_grad,
            first_row,
            0,
        )
        value_total = lax.dynamic_update_slice_in_dim(
            value_total,
            lax.dynamic_slice_in_dim(value_total, first_row, span_rows, 0) + value_grad,
            first_row,
            0,
        )
        sink_part = -jnp.sum(sink_share * row_delta, axis=1)
        return ((key_total, value_total), (query_grad, sink_part))

    initial = (
        jnp.zeros((reach_rows + seq_len, head_width), jnp.float32),
        jnp.zeros((reach_rows + seq_len, head_width), jnp.float32),
    )
    (key_total, value_total), (query_grad, sink_parts) = lax.scan(
        one_block, initial, jnp.arange(seq_len // block_rows, dtype=jnp.int32)
    )
    return (
        query_grad.reshape(seq_len, head_count, head_width),
        key_total[reach_rows:],
        value_total[reach_rows:],
        jnp.sum(sink_parts, axis=0),
    )


def inverse_of(slab_ids):
    count = slab_ids.shape[0]
    column = jnp.arange(count, dtype=jnp.int32)
    return jnp.sum(jnp.where(slab_ids[:, None] == column[None, :], column[:, None], 0), axis=0)


def to_natural(rows, inverse):
    count = inverse.shape[0]
    return rows.reshape(count, rows.shape[0] // count, rows.shape[1])[inverse].reshape(rows.shape)


def to_stored(rows, slab_ids):
    count = slab_ids.shape[0]
    return rows.reshape(count, rows.shape[0] // count, rows.shape[1])[slab_ids].reshape(rows.shape)


def on_device(queries, keys, values, grad_out, sink_logit, doc_lengths, slab_order):
    local_query = queries[0]
    local_grad = grad_out[0]
    local_key = keys[0]
    local_value = values[0]
    tok_rows = local_query.shape[0]
    head_width = HD
    wide_key = jnp.repeat(local_key.reshape(tok_rows, -1, head_width), 2, axis=1).reshape(
        tok_rows, -1
    )
    wide_value = jnp.repeat(local_value.reshape(tok_rows, -1, head_width), 2, axis=1).reshape(
        tok_rows, -1
    )
    head_query, head_grad, head_key, head_value = (
        lax.all_to_all(local_query, "ctx", split_axis=1, concat_axis=0, tiled=True),
        lax.all_to_all(local_grad, "ctx", split_axis=1, concat_axis=0, tiled=True),
        lax.all_to_all(wide_key, "ctx", split_axis=1, concat_axis=0, tiled=True),
        lax.all_to_all(wide_value, "ctx", split_axis=1, concat_axis=0, tiled=True),
    )
    seq_len = head_query.shape[0]
    slab_ids = slab_order[0]
    inverse = inverse_of(slab_ids)
    query_nat = to_natural(head_query, inverse).reshape(seq_len, -1, head_width)
    grad_nat = to_natural(head_grad, inverse).reshape(seq_len, -1, head_width)
    key_nat = to_natural(head_key, inverse)
    value_nat = to_natural(head_value, inverse)
    query_grad, key_grad, value_grad, sink_grad = head_group(
        query_nat, key_nat, value_nat, grad_nat, sink_logit, doc_lengths[0]
    )
    query_stored = to_stored(query_grad.reshape(seq_len, -1), slab_ids)
    key_stored = to_stored(key_grad, slab_ids)
    value_stored = to_stored(value_grad, slab_ids)
    grad_queries = lax.all_to_all(query_stored, "ctx", split_axis=0, concat_axis=1, tiled=True)
    back_key, back_value = (
        lax.all_to_all(key_stored, "ctx", split_axis=0, concat_axis=1, tiled=True),
        lax.all_to_all(value_stored, "ctx", split_axis=0, concat_axis=1, tiled=True),
    )
    grad_keys = (
        back_key.reshape(tok_rows, -1, 2, head_width)
        .sum(axis=2)
        .reshape(tok_rows, -1)
        .astype(jnp.bfloat16)
    )
    grad_values = (
        back_value.reshape(tok_rows, -1, 2, head_width)
        .sum(axis=2)
        .reshape(tok_rows, -1)
        .astype(jnp.bfloat16)
    )
    grad_sink = lax.psum(sink_grad, "dp")
    return (grad_queries[None], grad_keys[None], grad_values[None], grad_sink)


def solution(mesh):
    placed = (
        P("dp", "ctx", None),
        P("dp", "ctx", None),
        P("dp", "ctx", None),
        P("dp", "ctx", None),
        P("ctx"),
        P("dp", None),
        P("dp", None),
    )
    return jax.shard_map(
        on_device,
        mesh=mesh,
        in_specs=placed,
        out_specs=(P("dp", "ctx", None), P("dp", "ctx", None), P("dp", "ctx", None), P("ctx")),
        check_vma=False,
    )
```

profile of v0, /device:TPU:64, one launch (start us, length us, event | category | flops | bytes accessed | tf_op | source)
XLA Modules:
  0.0 356.8 jit_solution(18101805479335602170)
XLA Ops:
  2.7 10.0 %all-to-all-start = ((bf16[128,16,128]{2,0,1:T(8,128)(2,1)}), bf16[128,16,128]{2,0,1:T(8,128)(2,1)S(1)}, u32[]{:S(2)}, u32[]{:S(2)}) async-start(bf16[128,16,128]{2,0,1:T(8,128)(2,1)} %bitcast.15), calls=%async_computation | async-start | bytes 1048576 | tf_op jit(solution)/shard_map/all_to_all | solution.py:139
  13.7 13.3 %all-to-all-done = bf16[128,16,128]{2,0,1:T(8,128)(2,1)S(1)} async-done(((bf16[128,16,128]{2,0,1:T(8,128)(2,1)}), bf16[128,16,128]{2,0,1:T(8,128)(2,1)S(1)}, u32[]{:S(2)}, u32[]{:S(2)}) %all-to-all-start) | async-done | bytes 524320 | tf_op jit(solution)/shard_map/all_to_all | solution.py:139
  27.9 5.9 %all-to-all-start.2 = ((bf16[128,16,128]{2,0,1:T(8,128)(2,1)}), bf16[128,16,128]{2,0,1:T(8,128)(2,1)S(1)}, u32[]{:S(2)}, u32[]{:S(2)}) async-start(bf16[128,16,128]{2,0,1:T(8,128)(2,1)} %bitcast.25), calls=%async_computation.2 | async-start | bytes 1048576 | tf_op jit(solution)/shard_map/all_to_all | solution.py:140
  35.1 13.3 %all-to-all-done.2 = bf16[128,16,128]{2,0,1:T(8,128)(2,1)S(1)} async-done(((bf16[128,16,128]{2,0,1:T(8,128)(2,1)}), bf16[128,16,128]{2,0,1:T(8,128)(2,1)S(1)}, u32[]{:S(2)}, u32[]{:S(2)}) %all-to-all-start.2) | async-done | bytes 524320 | tf_op jit(solution)/shard_map/all_to_all | solution.py:140
  48.4 5.8 %all-to-all-start.1 = ((bf16[128,16,256]{0,2,1:T(8,128)(2,1)}), bf16[128,16,256]{0,2,1:T(8,128)(2,1)S(1)}, u32[]{:S(2)}, u32[]{:S(2)}) async-start(bf16[128,16,256]{0,2,1:T(8,128)(2,1)} %bitcast.22), calls=%async_computation.1 | async-start | bytes 2097152 | tf_op jit(solution)/shard_map/all_to_all | solution.py:137
  55.5 23.4 %all-to-all-done.1 = bf16[128,16,256]{0,2,1:T(8,128)(2,1)S(1)} async-done(((bf16[128,16,256]{0,2,1:T(8,128)(2,1)}), bf16[128,16,256]{0,2,1:T(8,128)(2,1)S(1)}, u32[]{:S(2)}, u32[]{:S(2)}) %all-to-all-start.1) | async-done | bytes 1048608 | tf_op jit(solution)/shard_map/all_to_all | solution.py:137
  78.9 6.7 %all-to-all-start.3 = ((bf16[128,16,256]{0,2,1:T(8,128)(2,1)}), bf16[128,16,256]{0,2,1:T(8,128)(2,1)S(1)}, u32[]{:S(2)}, u32[]{:S(2)}) async-start(bf16[128,16,256]{0,2,1:T(8,128)(2,1)} %bitcast.29), calls=%async_computation.3 | async-start | bytes 2097152 | tf_op jit(solution)/shard_map/all_to_all | solution.py:138
  86.7 1.4 gather_fusion
  88.8 1.9 concatenate.10
  93.9 16.4 %all-to-all-done.3 = bf16[128,16,256]{0,2,1:T(8,128)(2,1)S(1)} async-done(((bf16[128,16,256]{0,2,1:T(8,128)(2,1)}), bf16[128,16,256]{0,2,1:T(8,128)(2,1)S(1)}, u32[]{:S(2)}, u32[]{:S(2)}) %all-to-all-start.3) | async-done | bytes 1048608 | tf_op jit(solution)/shard_map/all_to_all | solution.py:138
  114.8 87.7 %while.18 = (s32[]{:T(128)}, f32[2304,128]{1,0:T(8,128)}, f32[2304,128]{1,0:T(8,128)}, bf16[4,512,2,128]{3,2,1,0:T(2,128)(2,1)}, f32[4,2]{1,0:T(4,128)}, /*index...) while((s32[]{:T(128)}, f32[2304,128]{1,0:T(8,128)}, ...), condition=%wide.region_8.9_spmd, body=%wide.region_3.8_spmd.sunk | while | flops 1229234432 | bytes 45857072 | solution.py:96
  116.6 1.4 constant_dynamic-slice_fusion.3
  118.8 1.7 fusion.70
  121.3 2.3 fusion.73
  125.8 2.9 fusion.76
  128.7 3.3 fusion.74
  132.0 1.4 fusion.77
  134.4 2.3 fusion.75
  138.6 1.4 constant_dynamic-slice_fusion.3
  140.7 1.7 fusion.70
  143.3 2.3 fusion.73
  147.7 2.9 fusion.76
  150.6 3.3 fusion.74
  156.3 2.3 fusion.75
  160.5 1.4 constant_dynamic-slice_fusion.3
  162.6 1.7 fusion.70
  165.2 2.3 fusion.73
  169.6 2.9 fusion.76
  172.6 3.3 fusion.74
  175.9 1.4 fusion.77
  178.3 2.3 fusion.75
  182.5 1.4 constant_dynamic-slice_fusion.3
  184.6 1.7 fusion.70
  187.1 2.3 fusion.73
  191.6 2.9 fusion.76
  194.5 3.2 fusion.74
  200.2 2.3 fusion.75
  202.6 1.8 reshape_reshape_reshape.3
  204.4 1.7 gather_fusion.4
  206.1 6.7 %all-to-all-start.4 = ((bf16[16,128,256]{2,1,0:T(8,128)(2,1)}), bf16[16,128,256]{2,1,0:T(8,128)(2,1)}, u32[]{:S(2)}, u32[]{:S(2)}) async-start(bf16[16,128,256]{2,1,0:T(8,128)(2,1)} %bitcast.34), calls=%async_computation.4 | async-start | bytes 2097152 | tf_op jit(solution)/shard_map/all_to_all | solution.py:155
  212.9 1.9 gather_fusion.5
  214.8 22.9 %all-to-all-done.4 = bf16[16,128,256]{2,1,0:T(8,128)(2,1)} async-done(((bf16[16,128,256]{2,1,0:T(8,128)(2,1)}), bf16[16,128,256]{2,1,0:T(8,128)(2,1)}, u32[]{:S(2)}, u32[]{:S(2)}) %all-to-all-start.4) | async-done | bytes 1048608 | tf_op jit(solution)/shard_map/all_to_all | solution.py:155
  237.7 6.7 %all-to-all-start.5 = ((f32[16,128,128]{2,1,0:T(8,128)}), f32[16,128,128]{2,1,0:T(8,128)S(1)}, u32[]{:S(2)}, u32[]{:S(2)}) async-start(f32[16,128,128]{2,1,0:T(8,128)} %bitcast.38), calls=%async_computation.5 | async-start | bytes 2097152 | tf_op jit(solution)/shard_map/all_to_all | solution.py:157
  244.5 1.8 gather_fusion.6
  246.3 22.9 %all-to-all-done.5 = f32[16,128,128]{2,1,0:T(8,128)S(1)} async-done(((f32[16,128,128]{2,1,0:T(8,128)}), f32[16,128,128]{2,1,0:T(8,128)S(1)}, u32[]{:S(2)}, u32[]{:S(2)}) %all-to-all-start.5) | async-done | bytes 1048608 | tf_op jit(solution)/shard_map/all_to_all | solution.py:157
  269.1 6.7 %all-to-all-start.6 = ((f32[16,128,128]{2,1,0:T(8,128)}), f32[16,128,128]{2,1,0:T(8,128)S(1)}, u32[]{:S(2)}, u32[]{:S(2)}) async-start(f32[16,128,128]{2,1,0:T(8,128)} %bitcast.43), calls=%async_computation.6 | async-start | bytes 2097152 | tf_op jit(solution)/shard_map/all_to_all | solution.py:158
  275.9 75.8 %psum.7 = f32[2]{0:T(128)} all-reduce(f32[2]{0:T(128)S(1)} %reduce_sum.88), channel_id=1, replica_groups=mesh['dp'=32,'ctx'=16] {'dp'}, use_global_device_ids=true, to_apply=%region_12.13 | all-reduce | flops 2 | bytes 16 | tf_op jit(solution)/shard_map/psum | solution.py:172
  351.7 1.6 copy.98
  (204 shorter events, 45.7 us)
Async XLA Ops:
  0.6 33.1 %copy-start.7 = (bf16[1,128,4096]{2,1,0:T(8,128)(2,1)S(1)}, bf16[1,128,4096]{2,1,0:T(8,128)(2,1)}, u32[]{:S(2)}) copy-start(bf16[1,128,4096]{2,1,0:T(8,128)(2,1)} %param.9) | copy-start | bytes 3145732
  2.7 24.3 %all-to-all-start = ((bf16[128,16,128]{2,0,1:T(8,128)(2,1)}), bf16[128,16,128]{2,0,1:T(8,128)(2,1)S(1)}, u32[]{:S(2)}, u32[]{:S(2)}) async-start(bf16[128,16,128]{2,0,1:T(8,128)(2,1)} %bitcast.15), calls=%async_computation | async-start | bytes 1048576 | tf_op jit(solution)/shard_map/all_to_all | solution.py:139
  13.7 40.4 %copy-start.8 = (bf16[1,128,4096]{2,1,0:T(8,128)(2,1)S(1)}, bf16[1,128,4096]{2,1,0:T(8,128)(2,1)}, u32[]{:S(2)}) copy-start(bf16[1,128,4096]{2,1,0:T(8,128)(2,1)} %param.12) | copy-start | bytes 3145732
  27.9 20.5 %all-to-all-start.2 = ((bf16[128,16,128]{2,0,1:T(8,128)(2,1)}), bf16[128,16,128]{2,0,1:T(8,128)(2,1)S(1)}, u32[]{:S(2)}, u32[]{:S(2)}) async-start(bf16[128,16,128]{2,0,1:T(8,128)(2,1)} %bitcast.25), calls=%async_computation.2 | async-start | bytes 1048576 | tf_op jit(solution)/shard_map/all_to_all | solution.py:140
  48.4 37.2 %copy-start.15 = (s32[1,16]{1,0:T(1,128)S(1)}, s32[1,16]{1,0:T(1,128)}, u32[]{:S(2)}) copy-start(s32[1,16]{1,0:T(1,128)} %param.14) | copy-start | bytes 196
  48.4 37.6 %copy-start.16 = (s32[1,32]{1,0:T(1,128)S(1)}, s32[1,32]{1,0:T(1,128)}, u32[]{:S(2)}) copy-start(s32[1,32]{1,0:T(1,128)} %param.15) | copy-start | bytes 388
  48.4 30.5 %all-to-all-start.1 = ((bf16[128,16,256]{0,2,1:T(8,128)(2,1)}), bf16[128,16,256]{0,2,1:T(8,128)(2,1)S(1)}, u32[]{:S(2)}, u32[]{:S(2)}) async-start(bf16[128,16,256]{0,2,1:T(8,128)(2,1)} %bitcast.22), calls=%async_computation.1 | async-start | bytes 2097152 | tf_op jit(solution)/shard_map/all_to_all | solution.py:137
  78.9 31.5 %all-to-all-start.3 = ((bf16[128,16,256]{0,2,1:T(8,128)(2,1)}), bf16[128,16,256]{0,2,1:T(8,128)(2,1)S(1)}, u32[]{:S(2)}, u32[]{:S(2)}) async-start(bf16[128,16,256]{0,2,1:T(8,128)(2,1)} %bitcast.29), calls=%async_computation.3 | async-start | bytes 2097152 | tf_op jit(solution)/shard_map/all_to_all | solution.py:138
  110.9 4.0 %copy-start.9 = (f32[2]{0:T(128)S(1)}, f32[2]{0:T(128)}, u32[]{:S(2)}) copy-start(f32[2]{0:T(128)} %param.13) | copy-start | bytes 28
  114.8 3.2 copy-start.10
  114.8 3.2 copy-start.12
  114.8 3.2 copy-start.17
  118.1 3.3 copy-start.4
  120.4 5.3 %copy-start = (f32[768,512,2]{1,0,2:T(8,128)}, f32[768,512,2]{1,0,2:T(8,128)S(1)}, u32[]{:S(2)}) copy-start(f32[768,512,2]{1,0,2:T(8,128)S(1)} %get-tuple-element.368) | copy-start | bytes 9437188 | tf_op jit(solution)/shard_map/while
  131.9 4.8 %copy-start.11 = (s32[2304]{0:T(1024)S(1)}, s32[2304]{0:T(1024)}, u32[]{:S(2)}) copy-start(s32[2304]{0:T(1024)} %copy-done.10) | copy-start | bytes 27652 | tf_op jit(solution)/shard_map/while
  131.9 4.8 %copy-start.13 = (s32[2048]{0:T(1024)S(1)}, s32[2048]{0:T(1024)}, u32[]{:S(2)}) copy-start(s32[2048]{0:T(1024)} %copy-done.12) | copy-start | bytes 24580 | tf_op jit(solution)/shard_map/while
  132.0 4.8 %copy-start.18 = (s32[4]{0:T(128)S(1)}, s32[4]{0:T(128)}, u32[]{:S(2)}) copy-start(s32[4]{0:T(128)} %copy-done.17) | copy-start | bytes 52 | tf_op jit(solution)/shard_map/while
  136.8 3.3 copy-start.10
  136.8 3.3 copy-start.12
  136.8 3.3 copy-start.17
  140.0 3.3 copy-start.4
  142.4 5.3 %copy-start = (f32[768,512,2]{1,0,2:T(8,128)}, f32[768,512,2]{1,0,2:T(8,128)S(1)}, u32[]{:S(2)}) copy-start(f32[768,512,2]{1,0,2:T(8,128)S(1)} %get-tuple-element.368) | copy-start | bytes 9437188 | tf_op jit(solution)/shard_map/while
  153.9 4.8 %copy-start.11 = (s32[2304]{0:T(1024)S(1)}, s32[2304]{0:T(1024)}, u32[]{:S(2)}) copy-start(s32[2304]{0:T(1024)} %copy-done.10) | copy-start | bytes 27652 | tf_op jit(solution)/shard_map/while
  153.9 4.8 %copy-start.13 = (s32[2048]{0:T(1024)S(1)}, s32[2048]{0:T(1024)}, u32[]{:S(2)}) copy-start(s32[2048]{0:T(1024)} %copy-done.12) | copy-start | bytes 24580 | tf_op jit(solution)/shard_map/while
  153.9 4.8 %copy-start.18 = (s32[4]{0:T(128)S(1)}, s32[4]{0:T(128)}, u32[]{:S(2)}) copy-start(s32[4]{0:T(128)} %copy-done.17) | copy-start | bytes 52 | tf_op jit(solution)/shard_map/while
  158.7 3.3 copy-start.10
  158.7 3.3 copy-start.12
  158.7 3.3 copy-start.17
  161.9 3.3 copy-start.4
  164.3 5.3 %copy-start = (f32[768,512,2]{1,0,2:T(8,128)}, f32[768,512,2]{1,0,2:T(8,128)S(1)}, u32[]{:S(2)}) copy-start(f32[768,512,2]{1,0,2:T(8,128)S(1)} %get-tuple-element.368) | copy-start | bytes 9437188 | tf_op jit(solution)/shard_map/while
  169.6 2.9 copy-start.5
  175.8 4.8 %copy-start.11 = (s32[2304]{0:T(1024)S(1)}, s32[2304]{0:T(1024)}, u32[]{:S(2)}) copy-start(s32[2304]{0:T(1024)} %copy-done.10) | copy-start | bytes 27652 | tf_op jit(solution)/shard_map/while
  175.8 4.8 %copy-start.13 = (s32[2048]{0:T(1024)S(1)}, s32[2048]{0:T(1024)}, u32[]{:S(2)}) copy-start(s32[2048]{0:T(1024)} %copy-done.12) | copy-start | bytes 24580 | tf_op jit(solution)/shard_map/while
  175.9 4.8 %copy-start.18 = (s32[4]{0:T(128)S(1)}, s32[4]{0:T(128)}, u32[]{:S(2)}) copy-start(s32[4]{0:T(128)} %copy-done.17) | copy-start | bytes 52 | tf_op jit(solution)/shard_map/while
  180.6 3.3 copy-start.10
  180.7 3.3 copy-start.12
  180.7 3.3 copy-start.17
  183.9 3.3 copy-start.4
  186.2 5.3 %copy-start = (f32[768,512,2]{1,0,2:T(8,128)}, f32[768,512,2]{1,0,2:T(8,128)S(1)}, u32[]{:S(2)}) copy-start(f32[768,512,2]{1,0,2:T(8,128)S(1)} %get-tuple-element.368) | copy-start | bytes 9437188 | tf_op jit(solution)/shard_map/while
  197.8 4.8 %copy-start.11 = (s32[2304]{0:T(1024)S(1)}, s32[2304]{0:T(1024)}, u32[]{:S(2)}) copy-start(s32[2304]{0:T(1024)} %copy-done.10) | copy-start | bytes 27652 | tf_op jit(solution)/shard_map/while
  197.8 4.8 %copy-start.13 = (s32[2048]{0:T(1024)S(1)}, s32[2048]{0:T(1024)}, u32[]{:S(2)}) copy-start(s32[2048]{0:T(1024)} %copy-done.12) | copy-start | bytes 24580 | tf_op jit(solution)/shard_map/while
  197.8 4.8 %copy-start.18 = (s32[4]{0:T(128)S(1)}, s32[4]{0:T(128)}, u32[]{:S(2)}) copy-start(s32[4]{0:T(128)} %copy-done.17) | copy-start | bytes 52 | tf_op jit(solution)/shard_map/while
  202.6 10.3 %copy-start.3 = (f32[2304,128]{1,0:T(8,128)S(1)}, f32[2304,128]{1,0:T(8,128)}, u32[]{:S(2)}) copy-start(f32[2304,128]{1,0:T(8,128)} %get-tuple-element.169) | copy-start | bytes 3538948
  206.1 31.6 %all-to-all-start.4 = ((bf16[16,128,256]{2,1,0:T(8,128)(2,1)}), bf16[16,128,256]{2,1,0:T(8,128)(2,1)}, u32[]{:S(2)}, u32[]{:S(2)}) async-start(bf16[16,128,256]{2,1,0:T(8,128)(2,1)} %bitcast.34), calls=%async_computation.4 | async-start | bytes 2097152 | tf_op jit(solution)/shard_map/all_to_all | solution.py:155
  212.8 31.6 %copy-start.6 = (f32[2304,128]{1,0:T(8,128)S(1)}, f32[2304,128]{1,0:T(8,128)}, u32[]{:S(2)}) copy-start(f32[2304,128]{1,0:T(8,128)} %get-tuple-element.170) | copy-start | bytes 3538948
  237.7 31.5 %all-to-all-start.5 = ((f32[16,128,128]{2,1,0:T(8,128)}), f32[16,128,128]{2,1,0:T(8,128)S(1)}, u32[]{:S(2)}, u32[]{:S(2)}) async-start(f32[16,128,128]{2,1,0:T(8,128)} %bitcast.38), calls=%async_computation.5 | async-start | bytes 2097152 | tf_op jit(solution)/shard_map/all_to_all | solution.py:157
  244.4 31.5 %copy-start.14 = (f32[4,2]{1,0:T(4,128)S(1)}, f32[4,2]{1,0:T(4,128)}, u32[]{:S(2)}) copy-start(f32[4,2]{1,0:T(4,128)} %get-tuple-element.171) | copy-start | bytes 100
  269.1 86.6 %all-to-all-start.6 = ((f32[16,128,128]{2,1,0:T(8,128)}), f32[16,128,128]{2,1,0:T(8,128)S(1)}, u32[]{:S(2)}, u32[]{:S(2)}) async-start(f32[16,128,128]{2,1,0:T(8,128)} %bitcast.43), calls=%async_computation.6 | async-start | bytes 2097152 | tf_op jit(solution)/shard_map/all_to_all | solution.py:158
  (11 other events, 21.5 us)
where the time goes:
time: 359 us; the launch traced here: 357 us
  waiting for transfers between devices  112 us (31%)
  blocking collectives  75.8 us (21%)
  matrix products  55.5 us (15%)
  local copies, waits for them, and re-layouts  51.3 us (14%)
  starting transfers between devices  48.4 us (13%)
  other arithmetic  9.38 us (3%)
    psum x1, blocking collectives, on_device(): grad_sink = lax.psum(sink_grad, 'dp')  75.8 us
    all_to_all x1, waiting for transfers between devices, on_device(): lax.all_to_all(local_query, 'ctx', split_axis=1, concat_axis=0, tiled=True)  23.4 us
    all_to_all x1, waiting for transfers between devices, on_device(): lax.all_to_all(query_stored, 'ctx', split_axis=0, concat_axis=1, tiled=True)  22.9 us
    all_to_all x1, waiting for transfers between devices, on_device(): lax.all_to_all(key_stored, 'ctx', split_axis=0, concat_axis=1, tiled=True)  22.9 us
    all_to_all x1, waiting for transfers between devices, on_device(): lax.all_to_all(local_grad, 'ctx', split_axis=1, concat_axis=0, tiled=True)  16.4 us
    all_to_all x1, waiting for transfers between devices, on_device(): lax.all_to_all(wide_key, 'ctx', split_axis=1, concat_axis=0, tiled=True)  13.3 us
    all_to_all x1, waiting for transfers between devices, on_device(): lax.all_to_all(wide_value, 'ctx', split_axis=1, concat_axis=0, tiled=True)  13.3 us
    dot_general x4, matrix products, one_block(): jnp.einsum('bhd,kd->hbk', grad_rows, value_rows, preferred_element_type=j...  13 us
  transfers between devices with their start and end apart: 7, of which 6 were waited for; matrix products, arithmetic and copies ran while one was open for 6% of the time, Pallas kernels for 0%

commit v1 on v0

v1 whole, which is shorter than its diff:
```python
import functools
import math

import jax
import jax.numpy as jnp
from jax import lax
from jax.experimental import pallas as pl
from jax.experimental.pallas import tpu as pltpu
from jax.sharding import PartitionSpec as P

HD = 128
SLAB = 64
REACH = 4
WIN = REACH + 1
FAR = -1e30
MESH = pl.DeviceIdType.MESH
F32 = jnp.float32
BF16 = jnp.bfloat16


def kernel(n_dp, n_ctx, order, lens, sink, q_hbm, k_hbm, v_hbm, g_hbm,
           gq_out, gk_out, gv_out, gs_out,
           kv0, kv1, kv2, kv3, q_buf, g_buf, gq_buf, terms, part, inbox, bias, fin,
           sink_own, sink_in, gs_own, gs_in, window, slot,
           load_sem, swap_send, swap_recv, qg_load, qg_send, qg_recv,
           ag_send, ag_recv, rs_send, rs_recv, gq_store, gq_send, gq_recv,
           fin_store, fin_send, fin_recv, s_send, s_recv, t_send, t_recv):
    kvs = (kv0, kv1, kv2, kv3)
    n_heads = len(kvs)
    n_z = n_ctx // 2
    per_chip = 4
    n_slabs = n_z * per_chip
    dp, ctx = lax.axis_index("dp"), lax.axis_index("ctx")
    z, core = ctx // 2, ctx % 2
    peer = 2 * z + 1 - core
    right = 2 * lax.rem(z + 1, n_z) + core
    left = 2 * lax.rem(z + n_z - 1, n_z) + core
    half = n_z // 2

    def xor(value, bit):
        return value + bit - 2 * bit * lax.rem(value // bit, 2)

    ctx_bits = [1 << i for i in range(n_ctx.bit_length() - 1)]
    dp_bits = [1 << i for i in range(n_dp.bit_length() - 1)]
    ctx_mates = [(dp, xor(ctx, bit)) for bit in ctx_bits]
    dp_mates = [(xor(dp, bit), ctx) for bit in dp_bits]

    barrier = pltpu.get_barrier_semaphore()
    greeted = [(dp, left), (dp, right)] + ctx_mates + dp_mates
    for mate in greeted:
        pl.semaphore_signal(barrier, inc=1, device_id=mate, device_id_type=MESH)

    wide = q_hbm.shape[2] // 2
    kw = k_hbm.shape[2] // 2
    mine = pl.ds(2 * ctx, 2)
    loads = []
    for k in range(n_heads):
        cols = pl.ds(pl.multiple_of(core * kw + k * HD, HD), HD)
        for t, src in enumerate((k_hbm, v_hbm)):
            copy = pltpu.make_async_copy(src.at[:, :, cols], kvs[k].at[t, mine], load_sem.at[k, t])
            copy.start()
            loads.append(copy)
    own_cols = pl.ds(pl.multiple_of(core * wide, HD), wide)
    peer_cols = pl.ds(pl.multiple_of((1 - core) * wide, HD), wide)
    own_rows = pl.ds(2 * core, 2)
    qg_loads = []
    for t, (src, dst) in enumerate(((q_hbm, q_buf), (g_hbm, g_buf))):
        copy = pltpu.make_async_copy(src.at[:, :, own_cols], dst.at[own_rows], qg_load.at[t])
        copy.start()
        qg_loads.append(copy)
    lane = lax.broadcasted_iota(jnp.int32, (1, HD), 1)
    sink_own[...] = jnp.zeros_like(sink_own)
    sink_own[pl.ds(ctx, 1), :] = jnp.where(lane < SLAB, sink[0], sink[1])

    pl.semaphore_wait(barrier, len(greeted))

    swaps = []
    for k in range(n_heads):
        cols = pl.ds(pl.multiple_of((1 - core) * kw + k * HD, HD), HD)
        for t, src in enumerate((k_hbm, v_hbm)):
            copy = pltpu.make_async_remote_copy(
                src.at[:, :, cols], kvs[k].at[t, mine], swap_send.at[k, t], swap_recv.at[k, t],
                device_id=(dp, peer), device_id_type=MESH)
            copy.start()
            swaps.append(copy)

    def chip_rows(z_of):
        return pl.ds(per_chip * z_of, per_chip)

    def gather(k, way, step):
        owner = lax.rem(z - (step - 1) + n_z, n_z) if way == 0 else lax.rem(z + step - 1, n_z)
        block = kvs[k].at[:, chip_rows(owner)] if step < half else kvs[k].at[way, chip_rows(owner)]
        return pltpu.make_async_remote_copy(
            block, block, ag_send.at[k, way, step - 1], ag_recv.at[k, way, step - 1],
            device_id=(dp, (right, left)[way]), device_id_type=MESH)

    for k in range(n_heads):
        for t in range(2):
            loads[2 * k + t].wait()
            swaps[2 * k + t].wait_recv()
        for way in range(2):
            gather(k, way, 1).start()

    qg_swaps = []
    for t, (src, dst) in enumerate(((q_hbm, q_buf), (g_hbm, g_buf))):
        copy = pltpu.make_async_remote_copy(
            src.at[:, :, peer_cols], dst.at[own_rows], qg_send.at[t], qg_recv.at[t],
            device_id=(dp, peer), device_id_type=MESH)
        copy.start()
        qg_swaps.append(copy)

    def exchange(own, slots, send, recv, at, mate):
        copy = pltpu.make_async_remote_copy(
            own, slots.at[at], send.at[at], recv.at[at], device_id=mate, device_id_type=MESH)
        copy.start()
        copy.wait()
        own[...] = own[...] + slots[at]

    places = [order[0, 4 * z + i] for i in range(per_chip)]
    for i in range(per_chip):
        for w in range(WIN):
            window[i * WIN + w] = 0

    def note_slab(j, carry):
        place = order[0, j]
        new = []
        for i in range(per_chip):
            w = place - places[i] + REACH
            slot[j * per_chip + i] = jnp.where((w >= 0) & (w < WIN), i * WIN + w, per_chip * WIN)
            for v in range(WIN):
                new.append(jnp.where(w == v, j, carry[i * WIN + v]))
        return tuple(new)

    found = lax.fori_loop(0, n_slabs, note_slab, (jnp.int32(0),) * (per_chip * WIN))
    for i in range(per_chip * WIN):
        window[i] = found[i]

    row = lax.rem(lane, SLAB)
    key = lax.broadcasted_iota(jnp.int32, (WIN * SLAB, HD), 0)
    for i in range(per_chip):
        here = places[i] * SLAB + row
        begin = jnp.zeros_like(here)
        end = jnp.int32(0)
        for d in range(lens.shape[1]):
            end = end + lens[0, d]
            begin = jnp.where(here >= end, end, begin)
        begin = begin - (places[i] - REACH) * SLAB
        allowed = (key >= begin) & (key <= row + REACH * SLAB)
        bias[i] = jnp.where(allowed, 0.0, FAR)

    for k in range(n_heads):
        terms[k, per_chip * WIN] = jnp.zeros_like(terms[k, per_chip * WIN])
    gs_own[...] = jnp.zeros_like(gs_own)

    for step in range(2, half + 1):
        for k in range(n_heads):
            for way in range(2):
                gather(k, way, step - 1).wait_recv()
                gather(k, way, step).start()
        if step == 2:
            for at, mate in enumerate(ctx_mates):
                exchange(sink_own, sink_in, s_send, s_recv, at, mate)

    factor = 1.0 / math.sqrt(HD)
    group = wide // HD // n_heads

    def attend(k, i):
        kv = kvs[k]
        keys = jnp.concatenate([kv[0, window[i * WIN + w]] for w in range(WIN)], axis=0)
        vals = jnp.concatenate([kv[1, window[i * WIN + w]] for w in range(WIN)], axis=0)
        spans = [pl.ds((k * group + h) * HD, HD) for h in range(group)]
        q = jnp.concatenate([q_buf[i, :, span] for span in spans], axis=0)
        g = jnp.concatenate([g_buf[i, :, span] for span in spans], axis=0)
        pairs = group // 2
        first = pairs * (n_heads * core + k)
        sinks = jnp.concatenate([sink_own[pl.ds(first + p, 1), :] for p in range(pairs)], axis=1)
        nt = (((1,), (1,)), ((), ()))
        scores = lax.dot_general(keys, q, nt, preferred_element_type=F32)
        grad_prob = lax.dot_general(vals, g, nt, preferred_element_type=F32)
        mask = bias[i]
        scores = scores * factor + jnp.concatenate([mask] * pairs, axis=1)
        peak = jnp.maximum(sinks, jnp.max(scores, axis=0, keepdims=True))
        weights = jnp.exp(scores - peak)
        sink_weight = jnp.exp(sinks - peak)
        total = sink_weight + jnp.sum(weights, axis=0, keepdims=True)
        inverse = 1.0 / total
        softmax = weights * inverse
        rounded = softmax.astype(BF16)
        delta = jnp.sum(rounded.astype(F32) * grad_prob, axis=0, keepdims=True)
        grad_score = (softmax * (grad_prob - delta)).astype(BF16)
        grad_key = jnp.dot(grad_score, q, preferred_element_type=F32) * factor
        grad_val = jnp.dot(rounded, g, preferred_element_type=F32)
        grad_query = lax.dot_general(
            grad_score, keys, (((0,), (0,)), ((), ())), preferred_element_type=F32) * factor
        for h in range(group):
            gq_buf[i, :, spans[h]] = grad_query[h * SLAB:(h + 1) * SLAB].astype(BF16)
        for w in range(WIN):
            terms[k, i * WIN + w, 0] = grad_key[w * SLAB:(w + 1) * SLAB]
            terms[k, i * WIN + w, 1] = grad_val[w * SLAB:(w + 1) * SLAB]
        share = sink_weight * inverse * delta
        for p in range(pairs):
            at = pl.ds(first + p, 1)
            gs_own[at, :] = gs_own[at, :] - share[:, p * HD:(p + 1) * HD]

    def own_terms(k, j, t):
        total = terms[k, slot[j * per_chip], t]
        for i in range(1, per_chip):
            total = total + terms[k, slot[j * per_chip + i], t]
        return total

    def reduced(k, way, step):
        far = half + 1 - step
        owner = lax.rem(z - far + n_z, n_z) if way == 0 else lax.rem(z + far, n_z)
        src, dst = part.at[k, :, chip_rows(owner)], inbox.at[k, way, step - 1]
        if step == 1:
            src, dst = part.at[k, way, chip_rows(owner)], inbox.at[k, way, step - 1, way]
        return owner, pltpu.make_async_remote_copy(
            src, dst, rs_send.at[k, way, step - 1], rs_recv.at[k, way, step - 1],
            device_id=(dp, (left, right)[way]), device_id_type=MESH)

    def sum_and_send(k, way, step):
        owner, copy = reduced(k, way, step)
        if step > 1:
            reduced(k, way, step - 1)[1].wait_recv()
        tensors = (way,) if step == 1 else (0, 1)

        def one(j, carry):
            for t in tensors:
                total = own_terms(k, per_chip * owner + j, t)
                if step > 2 or (step == 2 and t == way):
                    total = total + inbox[k, way, step - 2, t, j].astype(F32)
                part[k, t, per_chip * owner + j] = total.astype(BF16)
            return carry

        lax.fori_loop(0, per_chip, one, 0)
        copy.start()

    def gq_copies(k):
        cols = pl.ds(pl.multiple_of(core * wide + k * group * HD, HD), group * HD)
        here = pl.ds(k * group * HD, group * HD)
        keep = pltpu.make_async_copy(
            gq_buf.at[own_rows, :, here], gq_out.at[:, :, cols], gq_store.at[k])
        away = pltpu.make_async_remote_copy(
            gq_buf.at[pl.ds(2 - 2 * core, 2), :, here], gq_out.at[:, :, cols],
            gq_send.at[k], gq_recv.at[k], device_id=(dp, peer), device_id_type=MESH)
        return keep, away

    for t in range(2):
        qg_loads[t].wait()
        qg_swaps[t].wait_recv()
    for k in range(n_heads):
        for way in range(2):
            gather(k, way, half).wait_recv()

        def one_slab(i, carry, k=k):
            attend(k, i)
            return carry

        lax.fori_loop(0, per_chip, one_slab, 0)
        for way in range(2):
            sum_and_send(k, way, 1)
        for copy in gq_copies(k):
            copy.start()

    mates = ctx_mates[1:] + dp_mates + ctx_mates[:1]
    left_over = list(enumerate(mates))
    for step in range(2, half + 1):
        for k in range(n_heads):
            for way in range(2):
                sum_and_send(k, way, step)
            if left_over:
                at, mate = left_over.pop(0)
                exchange(gs_own, gs_in, t_send, t_recv, at, mate)
    for at, mate in left_over:
        exchange(gs_own, gs_in, t_send, t_recv, at, mate)

    sums = gs_own[pl.ds(ctx, 1), :]
    gs_out[0] = jnp.sum(jnp.where(lane < SLAB, sums, 0.0))
    gs_out[1] = jnp.sum(jnp.where(lane < SLAB, 0.0, sums))

    def fin_copies(k):
        cols = pl.ds(pl.multiple_of(core * kw + k * HD, HD), HD)
        copies = []
        for t, out in enumerate((gk_out, gv_out)):
            keep = pltpu.make_async_copy(
                fin.at[k, t, own_rows], out.at[:, :, cols], fin_store.at[k, t])
            away = pltpu.make_async_remote_copy(
                fin.at[k, t, pl.ds(2 - 2 * core, 2)], out.at[:, :, cols],
                fin_send.at[k, t], fin_recv.at[k, t], device_id=(dp, peer), device_id_type=MESH)
            copies.append((keep, away))
        return copies

    for k in range(n_heads):
        for way in range(2):
            reduced(k, way, half)[1].wait_recv()

        def last(j, carry, k=k):
            for t in range(2):
                total = own_terms(k, per_chip * z + j, t)
                for way in range(2):
                    total = total + inbox[k, way, half - 1, t, j].astype(F32)
                fin[k, t, j] = total.astype(BF16)
            return carry

        lax.fori_loop(0, per_chip, last, 0)
        for keep, away in fin_copies(k):
            keep.start()
            away.start()

    for copy in swaps + qg_swaps:
        copy.wait_send()
    for k in range(n_heads):
        for way in range(2):
            for step in range(1, half + 1):
                gather(k, way, step).wait_send()
                reduced(k, way, step)[1].wait_send()
        keep, away = gq_copies(k)
        keep.wait()
        away.wait()
        for keep, away in fin_copies(k):
            keep.wait()
            away.wait()


def on_device(n_dp, n_ctx, queries, keys, values, grad_out, sink_logit, doc_lengths, slab_order):
    def slabs(x):
        return x.reshape(2, SLAB, x.shape[2])

    n_heads, n_z, per_chip = 4, n_ctx // 2, 4
    n_slabs = n_z * per_chip
    wide = queries.shape[2] // 2
    n_pairs = 16
    half = n_z // 2
    n_s, n_t = n_ctx.bit_length() - 1, n_ctx.bit_length() - 1 + n_dp.bit_length() - 1
    dma = pltpu.SemaphoreType.DMA
    any_spec = pl.BlockSpec(memory_space=pl.ANY)
    smem = pl.BlockSpec(memory_space=pltpu.SMEM)
    kv = pltpu.VMEM((2, n_slabs, SLAB, HD), BF16)
    rows = pltpu.VMEM((per_chip, SLAB, wide), BF16)
    gq, gk, gv, gs = pl.pallas_call(
        functools.partial(kernel, n_dp, n_ctx),
        out_shape=(
            jax.ShapeDtypeStruct((2, SLAB, queries.shape[2]), BF16),
            jax.ShapeDtypeStruct((2, SLAB, keys.shape[2]), BF16),
            jax.ShapeDtypeStruct((2, SLAB, keys.shape[2]), BF16),
            jax.ShapeDtypeStruct((2,), F32),
        ),
        in_specs=[smem] * 3 + [any_spec] * 4,
        out_specs=(any_spec, any_spec, any_spec, smem),
        scratch_shapes=[
            kv, kv, kv, kv, rows, rows, rows,
            pltpu.VMEM((n_heads, per_chip * WIN + 1, 2, SLAB, HD), F32),
            pltpu.VMEM((n_heads, 2, n_slabs, SLAB, HD), BF16),
            pltpu.VMEM((n_heads, 2, half, 2, per_chip, SLAB, HD), BF16),
            pltpu.VMEM((per_chip, WIN * SLAB, HD), F32),
            pltpu.VMEM((n_heads, 2, per_chip, SLAB, HD), BF16),
            pltpu.VMEM((n_pairs, HD), F32),
            pltpu.VMEM((n_s, n_pairs, HD), F32),
            pltpu.VMEM((n_pairs, HD), F32),
            pltpu.VMEM((n_t, n_pairs, HD), F32),
            pltpu.SMEM((per_chip * WIN,), jnp.int32),
            pltpu.SMEM((n_slabs * per_chip,), jnp.int32),
            dma((n_heads, 2)), dma((n_heads, 2)), dma((n_heads, 2)),
            dma((2,)), dma((2,)), dma((2,)),
            dma((n_heads, 2, half)), dma((n_heads, 2, half)),
            dma((n_heads, 2, half)), dma((n_heads, 2, half)),
            dma((n_heads,)), dma((n_heads,)), dma((n_heads,)),
            dma((n_heads, 2)), dma((n_heads, 2)), dma((n_heads, 2)),
            dma((n_s,)), dma((n_s,)), dma((n_t,)), dma((n_t,)),
        ],
        compiler_params=pltpu.CompilerParams(
            collective_id=0, has_side_effects=True, vmem_limit_bytes=40 * 2**20),
        name="ring_attention",
    )(slab_order, doc_lengths, sink_logit, slabs(queries), slabs(keys), slabs(values), slabs(grad_out))
    return (gq.reshape(queries.shape), gk.reshape(keys.shape), gv.reshape(values.shape), gs)


def solution(mesh):
    rows = P("dp", "ctx", None)
    return jax.shard_map(
        functools.partial(on_device, mesh.shape["dp"], mesh.shape["ctx"]),
        mesh=mesh,
        in_specs=(rows, rows, rows, rows, P("ctx"), P("dp", None), P("dp", None)),
        out_specs=(rows, rows, rows, P("ctx")),
        check_vma=False,
    )
```

time: 359 us -> 136 us (0.38)
  the two profiles are of different devices: /device:TPU:64 before, /device:TPU:1 now
where the time goes in v1:
time: 136 us
  Pallas kernels  127 us (93%)
  local copies, waits for them, and re-layouts  7.9 us (6%)
    pallas_call x1, Pallas kernels, on_device(): pl.pallas_call(functools.partial(kernel, n_dp, n_ctx), out_shape=(jax.Sha...  127 us
    unnamed x18, local copies, waits for them, and re-layouts  7.9 us

profile of v1, /device:TPU:1, one launch (start us, length us, event | category | flops | bytes accessed | tf_op | source)
XLA Modules:
  0.0 135.7 jit_solution(9046328770245241222)
XLA Ops:
  0.6 0.0 copy-start.4
  0.6 0.0 copy-start.5
  0.7 0.0 copy-start.6
  0.7 0.6 copy-done.4
  1.3 0.0 copy-done.5
  1.3 0.0 copy-done.6
  1.3 0.0 copy-start
  1.3 1.2 copy-done
  2.5 0.0 copy-start.1
  2.5 1.2 copy-done.1
  3.8 0.0 copy-start.2
  3.8 0.9 copy-done.2
  4.7 0.0 copy-start.3
  4.7 0.9 copy-done.3
  5.7 127.2 %ring_attention.1 = (bf16[2,64,4096]{2,1,0:T(8,128)(2,1)S(1)}, bf16[2,64,1024]{2,1,0:T(8,128)(2,1)S(1)}, bf16[2,64,1024]{2,1,0:T(8,128)(2,1)S(1)}, f32[2]{0:T(128)S(1)}) custom-call(s32[1,32]{1,0:T(1,128)S(1)} %copy-done.4, s32[1,16]{1,0:T(1,128)S(1)} %copy-done.5, f32[2]{0:T(128)S(1)} %copy-done.6, bf16[2,64,4096]{2,1,0:T(8,128)(2,1)S(1)} %bitcast.7, ...), custom_call_target="tpu_custom_call" | custom-call | tf_op jit(solution)/shard_map/ring_attention/pallas_call | solution.py:340
  132.8 1.0 copy.15
  133.8 0.7 copy.16
  134.5 0.7 copy.17
  135.2 0.5 copy.18
Async XLA Ops:
  0.6 0.7 copy-start.4
  0.6 0.7 copy-start.5
  0.7 0.7 copy-start.6
  1.3 1.2 copy-start
  2.5 1.2 copy-start.1
  3.8 0.9 copy-start.2
  4.7 0.9 copy-start.3

commit v2 on v0

v2 whole, which is shorter than its diff:
```python
import functools
import math

import jax
import jax.numpy as jnp
from jax import lax
from jax.experimental import pallas as pl
from jax.experimental.pallas import tpu as pltpu
from jax.sharding import PartitionSpec as P

HD = 128
SLAB = 64
REACH = 4
WIN = REACH + 1
FAR = -1e30
MESH = pl.DeviceIdType.MESH
F32 = jnp.float32
BF16 = jnp.bfloat16

N_Z = 8
ARC = 6
PLACES = (0, 2, 4, 6)
UP, DOWN = 0, 1
SPARE = 3
PER_CHIP = 4
N_SLABS = N_Z * PER_CHIP
EMPTY = PER_CHIP * WIN

SENDS = {(UP, 0): 2, (UP, 2): 4, (UP, 4): 6, (DOWN, 2): 5, (DOWN, 4): 3, (DOWN, 6): 1}
GETS = {(UP, 0): 1, (UP, 2): 3, (UP, 4): 5, (DOWN, 0): 6, (DOWN, 2): 4, (DOWN, 4): 2}
GATHER_ORDER = ((DOWN, 6), (UP, 0), (DOWN, 4), (UP, 2), (DOWN, 2), (UP, 4))
REDUCE_MOST = {(UP, 0): 6, (DOWN, 4): 5, (UP, 2): 4, (DOWN, 2): 3, (UP, 4): 2, (DOWN, 0): 1}
REDUCE_ORDER = [(UP, 0, 6), (UP, 0, 5), (UP, 0, 4)]
for _d in range(6, 0, -1):
    for (_way, _b), _most in REDUCE_MOST.items():
        if _d <= _most and (_way, _b, _d) not in REDUCE_ORDER:
            REDUCE_ORDER.append((_way, _b, _d))


def facing(way, place):
    return (4 - place if way == UP else 6 - place) % 8


def kernel(n_dp, order, lens, sink, q_hbm, k_hbm, v_hbm, g_hbm,
           gq_out, gk_out, gv_out, gs_out,
           kv0, kv1, kv2, kv3, q_buf, g_buf, gq_buf, terms, part, inbox, bias, fin,
           sink_own, sink_in, gs_own, gs_in, window, slot,
           load_sem, swap_send, swap_recv, qg_load, qg_send, qg_recv, hand_send, hand_recv,
           ag_send, ag_recv, rs_send, rs_recv, gq_store, gq_send, gq_recv, back_send, back_recv,
           fin_store, fin_send, fin_recv, s_send, s_recv, t_send, t_recv):
    kvs = (kv0, kv1, kv2, kv3)
    dp, ctx = lax.axis_index("dp"), lax.axis_index("ctx")
    z, core = ctx // 2, lax.rem(ctx, 2)
    other = 1 - core
    peer = 2 * z + other
    sign = 1 - 2 * lax.rem(z + core, 2)

    def chip(distance):
        return lax.rem(z + sign * distance + 2 * N_Z, N_Z)

    up_chip, down_chip = chip(1), chip(-1)

    def head_of(of_core, place):
        flip = lax.rem(z + of_core, 2)
        return lax.rem(z - (place + flip * (5 - 2 * place)) + 2 * N_Z, N_Z)

    def device(of_chip, of_core):
        return (dp, 2 * of_chip + of_core)

    def xor(value, bit):
        return value + bit - 2 * bit * lax.rem(value // bit, 2)

    ctx_mates = [(dp, xor(ctx, bit)) for bit in (1, 2, 4, 8)]
    dp_mates = [(xor(dp, 1 << i), ctx) for i in range(n_dp.bit_length() - 1)]

    barrier = pltpu.get_barrier_semaphore()
    greeted = [device(c, k) for c in (up_chip, down_chip) for k in (core, other)]
    greeted += [ctx_mates[0], ctx_mates[2], ctx_mates[3]] + dp_mates
    for mate in greeted:
        pl.semaphore_signal(barrier, inc=1, device_id=mate, device_id_type=MESH)

    def remote(src, dst, send, recv, to):
        return pltpu.make_async_remote_copy(
            src, dst, send, recv, device_id=to, device_id_type=MESH)

    def columns(head, width):
        return pl.ds(pl.multiple_of(head * width, HD), width)

    group = q_hbm.shape[2] // k_hbm.shape[2]
    wide = group * HD
    mine = pl.ds(2 * ctx, 2)
    own_rows, other_rows = pl.ds(2 * core, 2), pl.ds(2 * other, 2)
    kv_hbm, qg_hbm, qg_buf = (k_hbm, v_hbm), (q_hbm, g_hbm), (q_buf, g_buf)

    loads = {}
    for u in (3, 0, 2, 1):
        cols = columns(head_of(core, 2 * u), HD)
        for t in range(2):
            loads[u, t] = pltpu.make_async_copy(
                kv_hbm[t].at[:, :, cols], kvs[u].at[t, mine], load_sem.at[u, t])
            loads[u, t].start()
    qg_loads = []
    for u in range(3):
        cols = columns(head_of(core, 2 * u), wide)
        for t in range(2):
            copy = pltpu.make_async_copy(
                qg_hbm[t].at[:, :, cols], qg_buf[t].at[u, own_rows], qg_load.at[u, t])
            copy.start()
            qg_loads.append(copy)
    lane = lax.broadcasted_iota(jnp.int32, (1, HD), 1)
    sink_own[...] = jnp.zeros_like(sink_own)
    sink_own[pl.ds(ctx, 1), :] = jnp.where(lane < SLAB, sink[0], sink[1])

    pl.semaphore_wait(barrier, len(greeted))

    swaps = {}
    for u in (3, 0, 2, 1):
        cols = columns(head_of(other, 2 * u), HD)
        for t in range(2):
            swaps[u, t] = remote(kv_hbm[t].at[:, :, cols], kvs[u].at[t, mine],
                                 swap_send.at[u, t], swap_recv.at[u, t], (dp, peer))
            swaps[u, t].start()

    def arrived_kv(u, t):
        theirs = pl.ds(2 * peer, 2)
        return remote(kvs[u].at[t, theirs], kvs[u].at[t, theirs],
                      swap_send.at[u, t], swap_recv.at[u, t], (dp, peer))

    def chip_rows(of_chip):
        return pl.ds(PER_CHIP * of_chip, PER_CHIP)

    def gather(way, place, step):
        source = chip_rows(chip(1 - step if way == UP else step - 1))
        to = facing(way, place)
        return remote(
            kvs[place // 2].at[:, source], kvs[to // 2].at[:, source],
            ag_send.at[place // 2, way, step - 1], ag_recv.at[to // 2, 1 - way, step - 1],
            device((up_chip, down_chip)[way], core))

    def gathered(way, place, step):
        source = chip_rows(chip(-step if way == UP else step))
        here = kvs[place // 2].at[:, source]
        return remote(here, here, ag_send.at[place // 2, way, step - 1],
                      ag_recv.at[place // 2, way, step - 1], (dp, peer))

    class Exchange:
        def __init__(self, own, slots, send, recv, mates):
            self.own, self.slots, self.send, self.recv = own, slots, send, recv
            self.todo = list(enumerate(mates))
            self.going = None

        def step(self):
            if self.going is not None:
                at, copy = self.going
                copy.wait()
                self.own[...] = self.own[...] + self.slots[at]
                self.going = None
            if self.todo:
                at, mate = self.todo.pop(0)
                copy = remote(self.own, self.slots.at[at], self.send.at[at], self.recv.at[at], mate)
                copy.start()
                self.going = (at, copy)

        def finish(self):
            while self.todo or self.going is not None:
                self.step()

    for way, place in GATHER_ORDER:
        u = place // 2
        if (u, 0) in loads:
            for t in range(2):
                loads.pop((u, t)).wait()
                arrived_kv(u, t).wait_recv()
        gather(way, place, 1).start()

    qg_swaps = []
    for u in range(3):
        cols = columns(head_of(other, 2 * u), wide)
        for t in range(2):
            copy = remote(qg_hbm[t].at[:, :, cols], qg_buf[t].at[u, own_rows],
                          qg_send.at[u, t], qg_recv.at[u, t], (dp, peer))
            copy.start()
            qg_swaps.append(copy)

    def arrived_qg(u, t):
        there = qg_buf[t].at[u, other_rows]
        return remote(there, there, qg_send.at[u, t], qg_recv.at[u, t], (dp, peer))

    def hand(rel, t):
        of_core, to = ((core, down_chip), (other, up_chip))[rel]
        cols = columns(head_of(of_core, 6), wide)
        return remote(qg_hbm[t].at[:, :, cols], qg_buf[t].at[SPARE, own_rows],
                      hand_send.at[rel, t], hand_recv.at[rel, t], device(to, of_core))

    def handed(rel, t):
        there = qg_buf[t].at[SPARE, (own_rows, other_rows)[rel]]
        return remote(there, there, hand_send.at[rel, t], hand_recv.at[rel, t], (dp, peer))

    row = lax.rem(lane, SLAB)
    key = lax.broadcasted_iota(jnp.int32, (WIN * SLAB, HD), 0)
    for e, of_chip in enumerate((z, down_chip)):
        places = [order[0, PER_CHIP * of_chip + i] for i in range(PER_CHIP)]

        def note_slab(j, carry, e=e, places=places):
            place = order[0, j]
            new = []
            for i in range(PER_CHIP):
                w = place - places[i] + REACH
                slot[(e * N_SLABS + j) * PER_CHIP + i] = jnp.where(
                    (w >= 0) & (w < WIN), i * WIN + w, EMPTY)
                for v in range(WIN):
                    new.append(jnp.where(w == v, j, carry[i * WIN + v]))
            return tuple(new)

        found = lax.fori_loop(0, N_SLABS, note_slab, (jnp.int32(0),) * EMPTY)
        for i in range(EMPTY):
            window[e * EMPTY + i] = found[i]
        for i in range(PER_CHIP):
            here = places[i] * SLAB + row
            begin = jnp.zeros_like(here)
            end = jnp.int32(0)
            for d in range(lens.shape[1]):
                end = end + lens[0, d]
                begin = jnp.where(here >= end, end, begin)
            begin = begin - (places[i] - REACH) * SLAB
            allowed = (key >= begin) & (key <= row + REACH * SLAB)
            bias[e, i] = jnp.where(allowed, 0.0, FAR)
    for u in range(4):
        terms[u, EMPTY] = jnp.zeros_like(terms[u, EMPTY])
    gs_own[...] = jnp.zeros_like(gs_own)

    factor = 1.0 / math.sqrt(HD)
    pairs = group // 2

    def attend(u, e, i):
        unit = SPARE if e else u
        kv = kvs[u]
        at = [window[e * EMPTY + i * WIN + w] for w in range(WIN)]
        keys = jnp.concatenate([kv[0, at[w]] for w in range(WIN)], axis=0)
        vals = jnp.concatenate([kv[1, at[w]] for w in range(WIN)], axis=0)
        q = jnp.concatenate([q_buf[unit, i, :, h * HD:(h + 1) * HD] for h in range(group)], axis=0)
        g = jnp.concatenate([g_buf[unit, i, :, h * HD:(h + 1) * HD] for h in range(group)], axis=0)
        first = pairs * head_of(core, 2 * u)
        sinks = jnp.concatenate([sink_own[pl.ds(first + p, 1), :] for p in range(pairs)], axis=1)
        nt = (((1,), (1,)), ((), ()))
        scores = lax.dot_general(keys, q, nt, preferred_element_type=F32)
        grad_prob = lax.dot_general(vals, g, nt, preferred_element_type=F32)
        scores = scores * factor + jnp.concatenate([bias[e, i]] * pairs, axis=1)
        peak = jnp.maximum(sinks, jnp.max(scores, axis=0, keepdims=True))
        weights = jnp.exp(scores - peak)
        sink_weight = jnp.exp(sinks - peak)
        total = sink_weight + jnp.sum(weights, axis=0, keepdims=True)
        inverse = 1.0 / total
        softmax = weights * inverse
        rounded = softmax.astype(BF16)
        delta = jnp.sum(rounded.astype(F32) * grad_prob, axis=0, keepdims=True)
        grad_score = (softmax * (grad_prob - delta)).astype(BF16)
        grad_key = jnp.dot(grad_score, q, preferred_element_type=F32) * factor
        grad_val = jnp.dot(rounded, g, preferred_element_type=F32)
        grad_query = lax.dot_general(
            grad_score, keys, (((0,), (0,)), ((), ())), preferred_element_type=F32) * factor
        for h in range(group):
            gq_buf[unit, i, :, h * HD:(h + 1) * HD] = grad_query[h * SLAB:(h + 1) * SLAB].astype(BF16)
        for w in range(WIN):
            terms[unit, i * WIN + w, 0] = grad_key[w * SLAB:(w + 1) * SLAB]
            terms[unit, i * WIN + w, 1] = grad_val[w * SLAB:(w + 1) * SLAB]
        share = sink_weight * inverse * delta
        for p in range(pairs):
            where = pl.ds(first + p, 1)
            gs_own[where, :] = gs_own[where, :] - share[:, p * HD:(p + 1) * HD]

    def attend_unit(u, e):
        def one(i, carry):
            attend(u, e, i)
            return carry

        lax.fori_loop(0, PER_CHIP, one, 0)

    def gq_copies(u):
        cols = columns(head_of(core, 2 * u), wide)
        return (pltpu.make_async_copy(gq_buf.at[u, own_rows], gq_out.at[:, :, cols], gq_store.at[u]),
                remote(gq_buf.at[u, other_rows], gq_out.at[:, :, cols],
                       gq_send.at[u], gq_recv.at[u], (dp, peer)))

    def gq_arrived(u):
        there = gq_out.at[:, :, columns(head_of(other, 2 * u), wide)]
        return remote(there, there, gq_send.at[u], gq_recv.at[u], (dp, peer))

    def gq_back(rel):
        to_core = (core, other)[rel]
        return remote(gq_buf.at[SPARE, (own_rows, other_rows)[rel]],
                      gq_out.at[:, :, columns(head_of(core, 0), wide)],
                      back_send.at[rel], back_recv.at[rel], device(down_chip, to_core))

    def gq_returned(rel):
        there = gq_out.at[:, :, columns(head_of((core, other)[rel], 6), wide)]
        return remote(there, there, back_send.at[rel], back_recv.at[rel], (dp, peer))

    sinks = Exchange(sink_own, sink_in, s_send, s_recv, ctx_mates)
    for step in range(2, ARC + 1):
        sinks.step()
        for way, place in GATHER_ORDER:
            if step <= SENDS[way, place]:
                gathered(way, place, step - 1).wait_recv()
                gather(way, place, step).start()
        if step == ARC - 1:
            for rel in range(2):
                for t in range(2):
                    hand(rel, t).start()
            sinks.finish()
            for copy in qg_loads:
                copy.wait()
            for u in range(3):
                for t in range(2):
                    arrived_qg(u, t).wait_recv()
            attend_unit(1, 0)
            for copy in gq_copies(1):
                copy.start()
    attend_unit(2, 0)
    for copy in gq_copies(2):
        copy.start()
    for step in range(1, ARC + 1):
        gathered(DOWN, 0, step).wait_recv()
    attend_unit(0, 0)
    for rel in range(2):
        for t in range(2):
            handed(rel, t).wait_recv()
    attend_unit(0, 1)

    def own_terms(u, j, t):
        total = terms[u, slot[j * PER_CHIP], t]
        for i in range(1, PER_CHIP):
            total = total + terms[u, slot[j * PER_CHIP + i], t]
        if u == 0:
            for i in range(PER_CHIP):
                total = total + terms[SPARE, slot[(N_SLABS + j) * PER_CHIP + i], t]
        return total

    def reduced(n):
        way, place, d = REDUCE_ORDER[n]
        to = facing(way, place)
        return remote(part.at[n], inbox.at[to // 2, 1 - way, d - 1],
                      rs_send.at[n], rs_recv.at[to // 2, 1 - way, d - 1],
                      device((up_chip, down_chip)[way], core))

    def came_in(way, place, d):
        here = inbox.at[place // 2, way, d]
        return remote(here, here, rs_send.at[0], rs_recv.at[place // 2, way, d], (dp, peer))

    sums = Exchange(gs_own, gs_in, t_send, t_recv, ctx_mates[1:] + dp_mates + ctx_mates[:1])
    for n, (way, place, d) in enumerate(REDUCE_ORDER):
        owner = chip(d if way == UP else -d)
        first = (way, place) == (UP, 0)
        if not first:
            came_in(way, place, d).wait_recv()

        def one(j, carry, n=n, way=way, place=place, d=d, owner=owner, first=first):
            for t in range(2):
                total = own_terms(place // 2, PER_CHIP * owner + j, t)
                if not first:
                    total = total + inbox[place // 2, way, d, t, j].astype(F32)
                part[n, t, j] = total.astype(BF16)
            return carry

        lax.fori_loop(0, PER_CHIP, one, 0)
        reduced(n).start()
        if n == 2:
            for rel in range(2):
                gq_back(rel).start()
            for copy in gq_copies(0):
                copy.start()
        if n >= 2 and n % 2 == 0:
            sums.step()
    sums.finish()

    totals = gs_own[pl.ds(ctx, 1), :]
    gs_out[0] = jnp.sum(jnp.where(lane < SLAB, totals, 0.0))
    gs_out[1] = jnp.sum(jnp.where(lane < SLAB, 0.0, totals))

    gkv_out = (gk_out, gv_out)

    def fin_copies(u, t):
        cols = columns(head_of(core, 2 * u), HD)
        src = fin.at[u, t] if u < 3 else inbox.at[3, UP, 0, t]
        return (pltpu.make_async_copy(src.at[own_rows], gkv_out[t].at[:, :, cols], fin_store.at[u, t]),
                remote(src.at[other_rows], gkv_out[t].at[:, :, cols],
                       fin_send.at[u, t], fin_recv.at[u, t], (dp, peer)))

    def fin_arrived(u, t):
        there = gkv_out[t].at[:, :, columns(head_of(other, 2 * u), HD)]
        return remote(there, there, fin_send.at[u, t], fin_recv.at[u, t], (dp, peer))

    for place, ways in ((6, (UP,)), (0, (DOWN,)), (2, (UP, DOWN)), (4, (UP, DOWN))):
        u = place // 2
        for way in ways:
            came_in(way, place, 0).wait_recv()
        if u < 3:
            def last(j, carry, u=u, ways=ways):
                for t in range(2):
                    total = own_terms(u, PER_CHIP * z + j, t)
                    for way in ways:
                        total = total + inbox[u, way, 0, t, j].astype(F32)
                    fin[u, t, j] = total.astype(BF16)
                return carry

            lax.fori_loop(0, PER_CHIP, last, 0)
        for t in range(2):
            for copy in fin_copies(u, t):
                copy.start()

    for copy in list(swaps.values()) + qg_swaps:
        copy.wait_send()
    for (way, place), count in SENDS.items():
        for step in range(1, count + 1):
            gather(way, place, step).wait_send()
    for n in range(len(REDUCE_ORDER)):
        reduced(n).wait_send()
    for rel in range(2):
        for t in range(2):
            hand(rel, t).wait_send()
        gq_back(rel).wait_send()
        gq_returned(rel).wait_recv()
    for u in range(3):
        keep, away = gq_copies(u)
        keep.wait()
        away.wait_send()
        gq_arrived(u).wait_recv()
    for u in (3, 0, 1, 2):
        for t in range(2):
            keep, away = fin_copies(u, t)
            keep.wait()
            away.wait_send()
            fin_arrived(u, t).wait_recv()


def on_device(n_dp, queries, keys, values, grad_out, sink_logit, doc_lengths, slab_order):
    def slabs(x):
        return x.reshape(2, SLAB, x.shape[2])

    wide = HD * (queries.shape[2] // keys.shape[2])
    n_t = 4 + n_dp.bit_length() - 1
    n_msgs = len(REDUCE_ORDER)
    dma = pltpu.SemaphoreType.DMA
    hbm = pl.BlockSpec(memory_space=pltpu.HBM)
    any_spec = pl.BlockSpec(memory_space=pl.ANY)
    smem = pl.BlockSpec(memory_space=pltpu.SMEM)
    kv = pltpu.VMEM((2, N_SLABS, SLAB, HD), BF16)
    rows = pltpu.VMEM((4, PER_CHIP, SLAB, wide), BF16)
    gq, gk, gv, gs = pl.pallas_call(
        functools.partial(kernel, n_dp),
        out_shape=(
            jax.ShapeDtypeStruct((2, SLAB, queries.shape[2]), BF16),
            jax.ShapeDtypeStruct((2, SLAB, keys.shape[2]), BF16),
            jax.ShapeDtypeStruct((2, SLAB, keys.shape[2]), BF16),
            jax.ShapeDtypeStruct((2,), F32),
        ),
        in_specs=[smem] * 3 + [hbm] * 4,
        out_specs=(any_spec, any_spec, any_spec, smem),
        scratch_shapes=[
            kv, kv, kv, kv, rows, rows, rows,
            pltpu.VMEM((4, EMPTY + 1, 2, SLAB, HD), F32),
            pltpu.VMEM((n_msgs, 2, PER_CHIP, SLAB, HD), BF16),
            pltpu.VMEM((4, 2, ARC, 2, PER_CHIP, SLAB, HD), BF16),
            pltpu.VMEM((2, PER_CHIP, WIN * SLAB, HD), F32),
            pltpu.VMEM((3, 2, PER_CHIP, SLAB, HD), BF16),
            pltpu.VMEM((16, HD), F32),
            pltpu.VMEM((4, 16, HD), F32),
            pltpu.VMEM((16, HD), F32),
            pltpu.VMEM((n_t, 16, HD), F32),
            pltpu.SMEM((2 * EMPTY,), jnp.int32),
            pltpu.SMEM((2 * N_SLABS * PER_CHIP,), jnp.int32),
            dma((4, 2)), dma((4, 2)), dma((4, 2)),
            dma((3, 2)), dma((3, 2)), dma((3, 2)), dma((2, 2)), dma((2, 2)),
            dma((4, 2, ARC)), dma((4, 2, ARC)),
            dma((n_msgs,)), dma((4, 2, ARC)),
            dma((3,)), dma((3,)), dma((3,)), dma((2,)), dma((2,)),
            dma((4, 2)), dma((4, 2)), dma((4, 2)),
            dma((4,)), dma((4,)), dma((n_t,)), dma((n_t,)),
        ],
        compiler_params=pltpu.CompilerParams(
            collective_id=0, has_side_effects=True, vmem_limit_bytes=40 * 2**20),
        name="arc_attention",
    )(slab_order, doc_lengths, sink_logit, slabs(queries), slabs(keys), slabs(values), slabs(grad_out))
    return (gq.reshape(queries.shape), gk.reshape(keys.shape), gv.reshape(values.shape), gs)


def solution(mesh):
    rows = P("dp", "ctx", None)
    return jax.shard_map(
        functools.partial(on_device, mesh.shape["dp"]),
        mesh=mesh,
        in_specs=(rows, rows, rows, rows, P("ctx"), P("dp", None), P("dp", None)),
        out_specs=(rows, rows, rows, P("ctx")),
        check_vma=False,
    )
```

time: 359 us -> 115 us (0.32)
  the two profiles are of different devices: /device:TPU:64 before, /device:TPU:1 now
where the time goes in v2:
time: 115 us
  Pallas kernels  106 us (92%)
  local copies, waits for them, and re-layouts  7.9 us (7%)
    pallas_call x1, Pallas kernels, on_device(): pl.pallas_call(functools.partial(kernel, n_dp), out_shape=(jax.ShapeDtype...  106 us
    unnamed x18, local copies, waits for them, and re-layouts  7.9 us

profile of v2, /device:TPU:1, one launch (start us, length us, event | category | flops | bytes accessed | tf_op | source)
XLA Modules:
  0.0 114.7 jit_solution(1804439303534775561)
XLA Ops:
  0.6 0.0 copy-start.4
  0.6 0.0 copy-start.5
  0.7 0.0 copy-start.6
  0.7 0.6 copy-done.4
  1.3 0.0 copy-done.5
  1.3 0.0 copy-done.6
  1.3 0.0 copy-start
  1.3 1.2 %copy-done = bf16[1,128,4096]{2,1,0:T(8,128)(2,1)S(1)} copy-done((bf16[1,128,4096]{2,1,0:T(8,128)(2,1)S(1)}, bf16[1,128,4096]{2,1,0:T(8,128)(2,1)}, u32[]{:S(2)}) %copy-start) | copy-done | bytes 1048600
  2.5 0.0 copy-start.1
  2.5 1.2 %copy-done.1 = bf16[1,128,4096]{2,1,0:T(8,128)(2,1)S(1)} copy-done((bf16[1,128,4096]{2,1,0:T(8,128)(2,1)S(1)}, bf16[1,128,4096]{2,1,0:T(8,128)(2,1)}, u32[]{:S(2)}) %copy-start.1) | copy-done | bytes 1048600
  3.8 0.0 copy-start.2
  3.8 0.9 copy-done.2
  4.7 0.0 copy-start.3
  4.7 0.9 copy-done.3
  5.7 106.2 %arc_attention.1 = (bf16[2,64,4096]{2,1,0:T(8,128)(2,1)S(1)}, bf16[2,64,1024]{2,1,0:T(8,128)(2,1)S(1)}, bf16[2,64,1024]{2,1,0:T(8,128)(2,1)S(1)}, f32[2]{0:T(128)S(1)}) custom-call(s32[1,32]{1,0:T(1,128)S(1)} %copy-done.4, s32[1,16]{1,0:T(1,128)S(1)} %copy-done.5, f32[2]{0:T(128)S(1)} %copy-done.6, bf16[2,64,4096]{2,1,0:T(8,128)(2,1)S(1)} %bitcast.7, ...), custom_call_target="tpu_custom_call" | custom-call | tf_op jit(solution)/shard_map/arc_attention/pallas_call | solution.py:449
  111.8 1.0 copy.15
  112.8 0.7 copy.16
  113.5 0.7 copy.17
  114.2 0.5 copy.18
Async XLA Ops:
  0.6 0.7 copy-start.4
  0.6 0.7 copy-start.5
  0.7 0.7 copy-start.6
  1.3 1.2 %copy-start = (bf16[1,128,4096]{2,1,0:T(8,128)(2,1)S(1)}, bf16[1,128,4096]{2,1,0:T(8,128)(2,1)}, u32[]{:S(2)}) copy-start(bf16[1,128,4096]{2,1,0:T(8,128)(2,1)} %param.7) | copy-start | bytes 3145732
  2.5 1.2 %copy-start.1 = (bf16[1,128,4096]{2,1,0:T(8,128)(2,1)S(1)}, bf16[1,128,4096]{2,1,0:T(8,128)(2,1)}, u32[]{:S(2)}) copy-start(bf16[1,128,4096]{2,1,0:T(8,128)(2,1)} %param.10) | copy-start | bytes 3145732
  3.8 0.9 copy-start.2
  4.7 0.9 copy-start.3

commit v3 on v2

--- a/solution.py
+++ b/solution.py
@@ -41,12 +41,17 @@
     return (4 - place if way == UP else 6 - place) % 8
 
 
-def kernel(n_dp, order, lens, sink, q_hbm, k_hbm, v_hbm, g_hbm,
+def dp_bits(n_dp):
+    bits = [1 << i for i in range(n_dp.bit_length() - 1)]
+    return [part for part in (bits[:2], bits[2:]) if part]
+
+
+def kernel(n_dp, order_hbm, lens_hbm, sink_hbm, q_hbm, k_hbm, v_hbm, g_hbm,
            gq_out, gk_out, gv_out, gs_out,
            kv0, kv1, kv2, kv3, q_buf, g_buf, gq_buf, terms, part, inbox, bias, fin,
-           sink_own, sink_in, gs_own, gs_in, window, slot,
-           load_sem, swap_send, swap_recv, qg_load, qg_send, qg_recv, hand_send, hand_recv,
-           ag_send, ag_recv, rs_send, rs_recv, gq_store, gq_send, gq_recv, back_send, back_recv,
+           sink_own, sink_in, gs_own, gs_in, order, lens, sink, window, slot,
+           small_sem, load_sem, swap_send, swap_recv, qg_load, qg_send, qg_recv, hand_send, hand_recv,
+           first_send, first_recv, ag_send, ag_recv, rs_send, rs_recv, gq_store, gq_send, gq_recv, back_send, back_recv,
            fin_store, fin_send, fin_recv, s_send, s_recv, t_send, t_recv):
     kvs = (kv0, kv1, kv2, kv3)
     dp, ctx = lax.axis_index("dp"), lax.axis_index("ctx")
@@ -70,12 +75,22 @@
     def xor(value, bit):
         return value + bit - 2 * bit * lax.rem(value // bit, 2)
 
-    ctx_mates = [(dp, xor(ctx, bit)) for bit in (1, 2, 4, 8)]
-    dp_mates = [(xor(dp, 1 << i), ctx) for i in range(n_dp.bit_length() - 1)]
+    def group(axis, bits):
+        mates = []
+        for pick in range(1, 1 << len(bits)):
+            at = {"dp": dp, "ctx": ctx}
+            for i, bit in enumerate(bits):
+                if pick >> i & 1:
+                    at[axis] = xor(at[axis], bit)
+            mates.append((at["dp"], at["ctx"]))
+        return mates
+
+    chip_pair, far_chips = group("ctx", (1, 2)), group("ctx", (4, 8))
+    dp_groups = [group("dp", bits) for bits in dp_bits(n_dp)]
 
     barrier = pltpu.get_barrier_semaphore()
     greeted = [device(c, k) for c in (up_chip, down_chip) for k in (core, other)]
-    greeted += [ctx_mates[0], ctx_mates[2], ctx_mates[3]] + dp_mates
+    greeted += chip_pair[:1] + far_chips + sum(dp_groups, [])
     for mate in greeted:
         pl.semaphore_signal(barrier, inc=1, device_id=mate, device_id_type=MESH)
 
@@ -86,45 +101,66 @@
     def columns(head, width):
         return pl.ds(pl.multiple_of(head * width, HD), width)
 
-    group = q_hbm.shape[2] // k_hbm.shape[2]
-    wide = group * HD
+    heads = q_hbm.shape[2] // k_hbm.shape[2]
+    wide = heads * HD
     mine = pl.ds(2 * ctx, 2)
     own_rows, other_rows = pl.ds(2 * core, 2), pl.ds(2 * other, 2)
     kv_hbm, qg_hbm, qg_buf = (k_hbm, v_hbm), (q_hbm, g_hbm), (q_buf, g_buf)
 
-    loads = {}
-    for u in (3, 0, 2, 1):
+    small = [pltpu.make_async_copy(src, dst, small_sem.at[i]) for i, (src, dst) in enumerate(
+        ((order_hbm, order), (lens_hbm, lens), (sink_hbm, sink)))]
+    for copy in small:
+        copy.start()
+    loads, swaps = [], []
+    for u in range(3):
         cols = columns(head_of(core, 2 * u), HD)
         for t in range(2):
-            loads[u, t] = pltpu.make_async_copy(
-                kv_hbm[t].at[:, :, cols], kvs[u].at[t, mine], load_sem.at[u, t])
-            loads[u, t].start()
-    qg_loads = []
+            loads.append(pltpu.make_async_copy(
+                kv_hbm[t].at[:, :, cols], kvs[u].at[t, mine], load_sem.at[u, t]))
+        cols = columns(head_of(core, 2 * u), wide)
+        for t in range(2):
+            loads.append(pltpu.make_async_copy(
+                qg_hbm[t].at[:, :, cols], qg_buf[t].at[u, own_rows], qg_load.at[u, t]))
+
+    pl.semaphore_wait(barrier, len(greeted))
+
+    def first(way, place, rel, t):
+        of_core = (core, other)[rel]
+        to = facing(way, place)
+        target = (up_chip, down_chip)[way ^ rel]
+        return remote(
+            kv_hbm[t].at[:, :, columns(head_of(of_core, place), HD)], kvs[to // 2].at[t, mine],
+            first_send.at[place // 2, way, rel, t], first_recv.at[to // 2, 1 - way, rel, t],
+            device(target, of_core))
+
+    for way, place in GATHER_ORDER:
+        for rel in range(2):
+            for t in range(2):
+                first(way, place, rel, t).start()
+
     for u in range(3):
-        cols = columns(head_of(core, 2 * u), wide)
-        for t in range(2):
-            copy = pltpu.make_async_copy(
-                qg_hbm[t].at[:, :, cols], qg_buf[t].at[u, own_rows], qg_load.at[u, t])
-            copy.start()
-            qg_loads.append(copy)
+        cols = columns(head_of(other, 2 * u), HD)
+        for t in range(2):
+            swaps.append(remote(kv_hbm[t].at[:, :, cols], kvs[u].at[t, mine],
+                                swap_send.at[u, t], swap_recv.at[u, t], (dp, peer)))
+        cols = columns(head_of(other, 2 * u), wide)
+        for t in range(2):
+            swaps.append(remote(qg_hbm[t].at[:, :, cols], qg_buf[t].at[u, own_rows],
+                                qg_send.at[u, t], qg_recv.at[u, t], (dp, peer)))
+    for copy in loads + swaps:
+        copy.start()
+
+    def arrived(u, t):
+        theirs = kvs[u].at[t, pl.ds(2 * peer, 2)]
+        there = qg_buf[t].at[u, other_rows]
+        return (remote(theirs, theirs, swap_send.at[u, t], swap_recv.at[u, t], (dp, peer)),
+                remote(there, there, qg_send.at[u, t], qg_recv.at[u, t], (dp, peer)))
+
+    for copy in small:
+        copy.wait()
     lane = lax.broadcasted_iota(jnp.int32, (1, HD), 1)
     sink_own[...] = jnp.zeros_like(sink_own)
-    sink_own[pl.ds(ctx, 1), :] = jnp.where(lane < SLAB, sink[0], sink[1])
-
-    pl.semaphore_wait(barrier, len(greeted))
-
-    swaps = {}
-    for u in (3, 0, 2, 1):
-        cols = columns(head_of(other, 2 * u), HD)
-        for t in range(2):
-            swaps[u, t] = remote(kv_hbm[t].at[:, :, cols], kvs[u].at[t, mine],
-                                 swap_send.at[u, t], swap_recv.at[u, t], (dp, peer))
-            swaps[u, t].start()
-
-    def arrived_kv(u, t):
-        theirs = pl.ds(2 * peer, 2)
-        return remote(kvs[u].at[t, theirs], kvs[u].at[t, theirs],
-                      swap_send.at[u, t], swap_recv.at[u, t], (dp, peer))
+    sink_own[pl.ds(ctx, 1), :] = jnp.where(lane < SLAB, sink[0, 0], sink[0, 1])
 
     def chip_rows(of_chip):
         return pl.ds(PER_CHIP * of_chip, PER_CHIP)
@@ -137,54 +173,44 @@
             ag_send.at[place // 2, way, step - 1], ag_recv.at[to // 2, 1 - way, step - 1],
             device((up_chip, down_chip)[way], core))
 
-    def gathered(way, place, step):
-        source = chip_rows(chip(-step if way == UP else step))
-        here = kvs[place // 2].at[:, source]
-        return remote(here, here, ag_send.at[place // 2, way, step - 1],
-                      ag_recv.at[place // 2, way, step - 1], (dp, peer))
+    def wait_gathered(way, place, step):
+        source = chip(-step if way == UP else step)
+        if step > 1:
+            here = kvs[place // 2].at[:, chip_rows(source)]
+            remote(here, here, ag_send.at[place // 2, way, step - 1],
+                   ag_recv.at[place // 2, way, step - 1], (dp, peer)).wait_recv()
+            return
+        for rel in range(2):
+            for t in range(2):
+                here = kvs[place // 2].at[t, pl.ds(2 * (2 * source + (core, other)[rel]), 2)]
+                remote(here, here, first_send.at[place // 2, way, rel, t],
+                       first_recv.at[place // 2, way, rel, t], (dp, peer)).wait_recv()
 
     class Exchange:
-        def __init__(self, own, slots, send, recv, mates):
+        def __init__(self, own, slots, send, recv, groups):
             self.own, self.slots, self.send, self.recv = own, slots, send, recv
-            self.todo = list(enumerate(mates))
-            self.going = None
+            self.todo, self.used, self.going = list(groups), 0, []
 
         def step(self):
-            if self.going is not None:
-                at, copy = self.going
-                copy.wait()
-                self.own[...] = self.own[...] + self.slots[at]
-                self.going = None
+            if self.going:
+                for _, copy in self.going:
+                    copy.wait()
+                values = [self.own[...]] + [self.slots[at] for at, _ in self.going]
+                while len(values) > 1:
+                    values = [values[i] + values[i + 1] for i in range(0, len(values), 2)]
+                self.own[...] = values[0]
+                self.going = []
             if self.todo:
-                at, mate = self.todo.pop(0)
-                copy = remote(self.own, self.slots.at[at], self.send.at[at], self.recv.at[at], mate)
-                copy.start()
-                self.going = (at, copy)
+                for mate in self.todo.pop(0):
+                    at = self.used
+                    copy = remote(self.own, self.slots.at[at], self.send.at[at], self.recv.at[at], mate)
+                    copy.start()
+                    self.going.append((at, copy))
+                    self.used += 1
 
         def finish(self):
-            while self.todo or self.going is not None:
+            while self.todo or self.going:
                 self.step()
-
-    for way, place in GATHER_ORDER:
-        u = place // 2
-        if (u, 0) in loads:
-            for t in range(2):
-                loads.pop((u, t)).wait()
-                arrived_kv(u, t).wait_recv()
-        gather(way, place, 1).start()
-
-    qg_swaps = []
-    for u in range(3):
-        cols = columns(head_of(other, 2 * u), wide)
-        for t in range(2):
-            copy = remote(qg_hbm[t].at[:, :, cols], qg_buf[t].at[u, own_rows],
-                          qg_send.at[u, t], qg_recv.at[u, t], (dp, peer))
-            copy.start()
-            qg_swaps.append(copy)
-
-    def arrived_qg(u, t):
-        there = qg_buf[t].at[u, other_rows]
-        return remote(there, there, qg_send.at[u, t], qg_recv.at[u, t], (dp, peer))
 
     def hand(rel, t):
         of_core, to = ((core, down_chip), (other, up_chip))[rel]
@@ -230,7 +256,7 @@
     gs_own[...] = jnp.zeros_like(gs_own)
 
     factor = 1.0 / math.sqrt(HD)
-    pairs = group // 2
+    pairs = heads // 2
 
     def attend(u, e, i):
         unit = SPARE if e else u
@@ -238,8 +264,8 @@
         at = [window[e * EMPTY + i * WIN + w] for w in range(WIN)]
         keys = jnp.concatenate([kv[0, at[w]] for w in range(WIN)], axis=0)
         vals = jnp.concatenate([kv[1, at[w]] for w in range(WIN)], axis=0)
-        q = jnp.concatenate([q_buf[unit, i, :, h * HD:(h + 1) * HD] for h in range(group)], axis=0)
-        g = jnp.concatenate([g_buf[unit, i, :, h * HD:(h + 1) * HD] for h in range(group)], axis=0)
+        q = jnp.concatenate([q_buf[unit, i, :, h * HD:(h + 1) * HD] for h in range(heads)], axis=0)
+        g = jnp.concatenate([g_buf[unit, i, :, h * HD:(h + 1) * HD] for h in range(heads)], axis=0)
         first = pairs * head_of(core, 2 * u)
         sinks = jnp.concatenate([sink_own[pl.ds(first + p, 1), :] for p in range(pairs)], axis=1)
         nt = (((1,), (1,)), ((), ()))
@@ -259,7 +285,7 @@
         grad_val = jnp.dot(rounded, g, preferred_element_type=F32)
         grad_query = lax.dot_general(
             grad_score, keys, (((0,), (0,)), ((), ())), preferred_element_type=F32) * factor
-        for h in range(group):
+        for h in range(heads):
             gq_buf[unit, i, :, h * HD:(h + 1) * HD] = grad_query[h * SLAB:(h + 1) * SLAB].astype(BF16)
         for w in range(WIN):
             terms[unit, i * WIN + w, 0] = grad_key[w * SLAB:(w + 1) * SLAB]
@@ -270,11 +296,8 @@
             gs_own[where, :] = gs_own[where, :] - share[:, p * HD:(p + 1) * HD]
 
     def attend_unit(u, e):
-        def one(i, carry):
+        for i in range(PER_CHIP):
             attend(u, e, i)
-            return carry
-
-        lax.fori_loop(0, PER_CHIP, one, 0)
 
     def gq_copies(u):
         cols = columns(head_of(core, 2 * u), wide)
@@ -296,31 +319,34 @@
         there = gq_out.at[:, :, columns(head_of((core, other)[rel], 6), wide)]
         return remote(there, there, back_send.at[rel], back_recv.at[rel], (dp, peer))
 
-    sinks = Exchange(sink_own, sink_in, s_send, s_recv, ctx_mates)
+    sinks = Exchange(sink_own, sink_in, s_send, s_recv, [far_chips, chip_pair])
     for step in range(2, ARC + 1):
-        sinks.step()
+        if step in (2, 4):
+            sinks.step()
         for way, place in GATHER_ORDER:
             if step <= SENDS[way, place]:
-                gathered(way, place, step - 1).wait_recv()
+                wait_gathered(way, place, step - 1)
                 gather(way, place, step).start()
         if step == ARC - 1:
             for rel in range(2):
-                for t in range(2):
-                    hand(rel, t).start()
+                hand(rel, 0).start()
             sinks.finish()
-            for copy in qg_loads:
+            for copy in loads:
                 copy.wait()
             for u in range(3):
                 for t in range(2):
-                    arrived_qg(u, t).wait_recv()
+                    for copy in arrived(u, t):
+                        copy.wait_recv()
             attend_unit(1, 0)
             for copy in gq_copies(1):
                 copy.start()
+    for rel in range(2):
+        hand(rel, 1).start()
     attend_unit(2, 0)
     for copy in gq_copies(2):
         copy.start()
     for step in range(1, ARC + 1):
-        gathered(DOWN, 0, step).wait_recv()
+        wait_gathered(DOWN, 0, step)
     attend_unit(0, 0)
     for rel in range(2):
         for t in range(2):
@@ -347,17 +373,17 @@
         here = inbox.at[place // 2, way, d]
         return remote(here, here, rs_send.at[0], rs_recv.at[place // 2, way, d], (dp, peer))
 
-    sums = Exchange(gs_own, gs_in, t_send, t_recv, ctx_mates[1:] + dp_mates + ctx_mates[:1])
+    sums = Exchange(gs_own, gs_in, t_send, t_recv, [far_chips, chip_pair] + dp_groups)
     for n, (way, place, d) in enumerate(REDUCE_ORDER):
         owner = chip(d if way == UP else -d)
-        first = (way, place) == (UP, 0)
-        if not first:
+        starts = (way, place) == (UP, 0)
+        if not starts:
             came_in(way, place, d).wait_recv()
 
-        def one(j, carry, n=n, way=way, place=place, d=d, owner=owner, first=first):
+        def one(j, carry, n=n, way=way, place=place, d=d, owner=owner, starts=starts):
             for t in range(2):
                 total = own_terms(place // 2, PER_CHIP * owner + j, t)
-                if not first:
+                if not starts:
                     total = total + inbox[place // 2, way, d, t, j].astype(F32)
                 part[n, t, j] = total.astype(BF16)
             return carry
@@ -369,7 +395,7 @@
                 gq_back(rel).start()
             for copy in gq_copies(0):
                 copy.start()
-        if n >= 2 and n % 2 == 0:
+        if n >= 2 and n % 4 == 2:
             sums.step()
     sums.finish()
 
@@ -408,10 +434,13 @@
             for copy in fin_copies(u, t):
                 copy.start()
 
-    for copy in list(swaps.values()) + qg_swaps:
+    for copy in swaps:
         copy.wait_send()
     for (way, place), count in SENDS.items():
-        for step in range(1, count + 1):
+        for rel in range(2):
+            for t in range(2):
+                first(way, place, rel, t).wait_send()
+        for step in range(2, count + 1):
             gather(way, place, step).wait_send()
     for n in range(len(REDUCE_ORDER)):
         reduced(n).wait_send()
@@ -438,7 +467,7 @@
         return x.reshape(2, SLAB, x.shape[2])
 
     wide = HD * (queries.shape[2] // keys.shape[2])
-    n_t = 4 + n_dp.bit_length() - 1
+    n_t = 6 + sum((1 << len(bits)) - 1 for bits in dp_bits(n_dp))
     n_msgs = len(REDUCE_ORDER)
     dma = pltpu.SemaphoreType.DMA
     hbm = pl.BlockSpec(memory_space=pltpu.HBM)
@@ -454,7 +483,7 @@
             jax.ShapeDtypeStruct((2, SLAB, keys.shape[2]), BF16),
             jax.ShapeDtypeStruct((2,), F32),
         ),
-        in_specs=[smem] * 3 + [hbm] * 4,
+        in_specs=[hbm] * 7,
         out_specs=(any_spec, any_spec, any_spec, smem),
         scratch_shapes=[
             kv, kv, kv, kv, rows, rows, rows,
@@ -464,23 +493,28 @@
             pltpu.VMEM((2, PER_CHIP, WIN * SLAB, HD), F32),
             pltpu.VMEM((3, 2, PER_CHIP, SLAB, HD), BF16),
             pltpu.VMEM((16, HD), F32),
-            pltpu.VMEM((4, 16, HD), F32),
+            pltpu.VMEM((6, 16, HD), F32),
             pltpu.VMEM((16, HD), F32),
             pltpu.VMEM((n_t, 16, HD), F32),
+            pltpu.SMEM(slab_order.shape, jnp.int32),
+            pltpu.SMEM(doc_lengths.shape, jnp.int32),
+            pltpu.SMEM((1, 2), F32),
             pltpu.SMEM((2 * EMPTY,), jnp.int32),
             pltpu.SMEM((2 * N_SLABS * PER_CHIP,), jnp.int32),
-            dma((4, 2)), dma((4, 2)), dma((4, 2)),
+            dma((3,)), dma((3, 2)), dma((3, 2)), dma((3, 2)),
             dma((3, 2)), dma((3, 2)), dma((3, 2)), dma((2, 2)), dma((2, 2)),
+            dma((4, 2, 2, 2)), dma((4, 2, 2, 2)),
             dma((4, 2, ARC)), dma((4, 2, ARC)),
             dma((n_msgs,)), dma((4, 2, ARC)),
             dma((3,)), dma((3,)), dma((3,)), dma((2,)), dma((2,)),
             dma((4, 2)), dma((4, 2)), dma((4, 2)),
-            dma((4,)), dma((4,)), dma((n_t,)), dma((n_t,)),
+            dma((6,)), dma((6,)), dma((n_t,)), dma((n_t,)),
         ],
         compiler_params=pltpu.CompilerParams(
             collective_id=0, has_side_effects=True, vmem_limit_bytes=40 * 2**20),
         name="arc_attention",
-    )(slab_order, doc_lengths, sink_logit, slabs(queries), slabs(keys), slabs(values), slabs(grad_out))
+    )(*[pltpu.with_memory_space_constraint(x, pltpu.HBM) for x in (
+        slab_order, doc_lengths, sink_logit[None], *map(slabs, (queries, keys, values, grad_out)))])
     return (gq.reshape(queries.shape), gk.reshape(keys.shape), gv.reshape(values.shape), gs)
 
 

time: 115 us -> 101 us (0.88)
  Pallas kernels: 106 us -> 97 us
  local copies, waits for them, and re-layouts: 7.9 us -> 2.89 us
    pallas_call x1, Pallas kernels: 106 us -> 97 us  [on_device(): pl.pallas_call(functools.partial(kernel, n_dp), out_shape=(jax.ShapeDtype...]
    unnamed x18 -> x4, local copies, waits for them, and re-layouts: 7.9 us -> 2.89 us
where the time goes in v3:
time: 101 us
  Pallas kernels  97 us (96%)
  local copies, waits for them, and re-layouts  2.89 us (3%)
    pallas_call x1, Pallas kernels, on_device(): pl.pallas_call(functools.partial(kernel, n_dp), out_shape=(jax.ShapeDtype...  97 us
    unnamed x4, local copies, waits for them, and re-layouts  2.89 us

profile of v3, /device:TPU:1, one launch (start us, length us, event | category | flops | bytes accessed | tf_op | source)
XLA Modules:
  0.0 100.5 jit_solution(15290817275228852829)
XLA Ops:
  0.6 97.0 %arc_attention.1 = (bf16[2,64,4096]{2,1,0:T(8,128)(2,1)S(1)}, bf16[2,64,1024]{2,1,0:T(8,128)(2,1)S(1)}, bf16[2,64,1024]{2,1,0:T(8,128)(2,1)S(1)}, f32[2]{0:T(128)S(1)}) custom-call(s32[1,32]{1,0:T(1,128)} %order_hbm.1, s32[1,16]{1,0:T(1,128)} %lens_hbm.1, f32[1,2]{1,0:T(1,128)} %bitcast.15, bf16[2,64,4096]{2,1,0:T(8,128)(2,1)} %bitcast.11, ...), custom_call_target="tpu_custom_call" | custom-call | tf_op jit(solution)/shard_map/arc_attention/pallas_call | solution.py:478
  97.7 1.0 copy.15
  98.6 0.7 copy.16
  99.3 0.7 copy.17
  100.0 0.5 copy.18

commit v4 on v3

--- a/solution.py
+++ b/solution.py
@@ -48,9 +48,9 @@
 
 def kernel(n_dp, order_hbm, lens_hbm, sink_hbm, q_hbm, k_hbm, v_hbm, g_hbm,
            gq_out, gk_out, gv_out, gs_out,
-           kv0, kv1, kv2, kv3, q_buf, g_buf, gq_buf, terms, part, inbox, bias, fin,
+           kv0, kv1, kv2, kv3, q_buf, g_buf, gq_buf, terms, ahead, rest, part, inbox, bias, fin,
            sink_own, sink_in, gs_own, gs_in, order, lens, sink, window, slot,
-           small_sem, load_sem, swap_send, swap_recv, qg_load, qg_send, qg_recv, hand_send, hand_recv,
+           hello, small_sem, load_sem, swap_send, swap_recv, qg_load, qg_send, qg_recv, hand_send, hand_recv,
            first_send, first_recv, ag_send, ag_recv, rs_send, rs_recv, gq_store, gq_send, gq_recv, back_send, back_recv,
            fin_store, fin_send, fin_recv, s_send, s_recv, t_send, t_recv):
     kvs = (kv0, kv1, kv2, kv3)
@@ -88,11 +88,20 @@
     chip_pair, far_chips = group("ctx", (1, 2)), group("ctx", (4, 8))
     dp_groups = [group("dp", bits) for bits in dp_bits(n_dp)]
 
+    dp_mates = []
+    for mates in dp_groups:
+        for pick, mate in enumerate(mates, 1):
+            dp_mates.append((mate, jnp.where(mate[0] > dp, 1, 0)))
+    higher = sum([above for _, above in dp_mates], jnp.int32(0))
     barrier = pltpu.get_barrier_semaphore()
     greeted = [device(c, k) for c in (up_chip, down_chip) for k in (core, other)]
-    greeted += chip_pair[:1] + far_chips + sum(dp_groups, [])
+    greeted += chip_pair[:1] + far_chips
     for mate in greeted:
         pl.semaphore_signal(barrier, inc=1, device_id=mate, device_id_type=MESH)
+    for mate, above in dp_mates:
+        @pl.when(above == 1)
+        def _(mate=mate):
+            pl.semaphore_signal(barrier, inc=1, device_id=mate, device_id_type=MESH)
 
     def remote(src, dst, send, recv, to):
         return pltpu.make_async_remote_copy(
@@ -122,7 +131,11 @@
             loads.append(pltpu.make_async_copy(
                 qg_hbm[t].at[:, :, cols], qg_buf[t].at[u, own_rows], qg_load.at[u, t]))
 
-    pl.semaphore_wait(barrier, len(greeted))
+    pl.semaphore_wait(barrier, len(greeted) + len(dp_mates) - higher)
+    for mate, above in dp_mates:
+        @pl.when(above == 0)
+        def _(mate=mate):
+            pl.semaphore_signal(hello, inc=1, device_id=mate, device_id_type=MESH)
 
     def first(way, place, rel, t):
         of_core = (core, other)[rel]
@@ -258,19 +271,22 @@
     factor = 1.0 / math.sqrt(HD)
     pairs = heads // 2
 
-    def attend(u, e, i):
+    nt = (((1,), (1,)), ((), ()))
+
+    def scores_of(u, e, i):
         unit = SPARE if e else u
-        kv = kvs[u]
         at = [window[e * EMPTY + i * WIN + w] for w in range(WIN)]
-        keys = jnp.concatenate([kv[0, at[w]] for w in range(WIN)], axis=0)
-        vals = jnp.concatenate([kv[1, at[w]] for w in range(WIN)], axis=0)
+        keys = jnp.concatenate([kvs[u][0, at[w]] for w in range(WIN)], axis=0)
+        vals = jnp.concatenate([kvs[u][1, at[w]] for w in range(WIN)], axis=0)
         q = jnp.concatenate([q_buf[unit, i, :, h * HD:(h + 1) * HD] for h in range(heads)], axis=0)
         g = jnp.concatenate([g_buf[unit, i, :, h * HD:(h + 1) * HD] for h in range(heads)], axis=0)
+        scores = lax.dot_general(keys, q, nt, preferred_element_type=F32)
+        grad_prob = lax.dot_general(vals, g, nt, preferred_element_type=F32)
+        return keys, q, g, scores, grad_prob
+
+    def softmax_of(u, e, i, scores, grad_prob):
         first = pairs * head_of(core, 2 * u)
         sinks = jnp.concatenate([sink_own[pl.ds(first + p, 1), :] for p in range(pairs)], axis=1)
-        nt = (((1,), (1,)), ((), ()))
-        scores = lax.dot_general(keys, q, nt, preferred_element_type=F32)
-        grad_prob = lax.dot_general(vals, g, nt, preferred_element_type=F32)
         scores = scores * factor + jnp.concatenate([bias[e, i]] * pairs, axis=1)
         peak = jnp.maximum(sinks, jnp.max(scores, axis=0, keepdims=True))
         weights = jnp.exp(scores - peak)
@@ -281,6 +297,14 @@
         rounded = softmax.astype(BF16)
         delta = jnp.sum(rounded.astype(F32) * grad_prob, axis=0, keepdims=True)
         grad_score = (softmax * (grad_prob - delta)).astype(BF16)
+        share = sink_weight * inverse * delta
+        for p in range(pairs):
+            where = pl.ds(first + p, 1)
+            gs_own[where, :] = gs_own[where, :] - share[:, p * HD:(p + 1) * HD]
+        return rounded, grad_score
+
+    def grads_of(u, e, i, keys, q, g, rounded, grad_score):
+        unit = SPARE if e else u
         grad_key = jnp.dot(grad_score, q, preferred_element_type=F32) * factor
         grad_val = jnp.dot(rounded, g, preferred_element_type=F32)
         grad_query = lax.dot_general(
@@ -290,14 +314,12 @@
         for w in range(WIN):
             terms[unit, i * WIN + w, 0] = grad_key[w * SLAB:(w + 1) * SLAB]
             terms[unit, i * WIN + w, 1] = grad_val[w * SLAB:(w + 1) * SLAB]
-        share = sink_weight * inverse * delta
-        for p in range(pairs):
-            where = pl.ds(first + p, 1)
-            gs_own[where, :] = gs_own[where, :] - share[:, p * HD:(p + 1) * HD]
 
     def attend_unit(u, e):
+        made = [scores_of(u, e, i) for i in range(PER_CHIP)]
+        probs = [softmax_of(u, e, i, *made[i][3:]) for i in range(PER_CHIP)]
         for i in range(PER_CHIP):
-            attend(u, e, i)
+            grads_of(u, e, i, *made[i][:3], *probs[i])
 
     def gq_copies(u):
         cols = columns(head_of(core, 2 * u), wide)
@@ -377,26 +399,44 @@
     for n, (way, place, d) in enumerate(REDUCE_ORDER):
         owner = chip(d if way == UP else -d)
         starts = (way, place) == (UP, 0)
+
+        def own(j, carry, n=n, place=place, owner=owner, starts=starts):
+            for t in range(2):
+                total = own_terms(place // 2, PER_CHIP * owner + j, t)
+                if starts:
+                    part[n, t, j] = total.astype(BF16)
+                else:
+                    ahead[t, j] = total
+            return carry
+
+        def add(j, carry, n=n, way=way, place=place, d=d):
+            for t in range(2):
+                part[n, t, j] = (ahead[t, j] + inbox[place // 2, way, d, t, j].astype(F32)).astype(BF16)
+            return carry
+
+        lax.fori_loop(0, PER_CHIP, own, 0)
         if not starts:
             came_in(way, place, d).wait_recv()
-
-        def one(j, carry, n=n, way=way, place=place, d=d, owner=owner, starts=starts):
-            for t in range(2):
-                total = own_terms(place // 2, PER_CHIP * owner + j, t)
-                if not starts:
-                    total = total + inbox[place // 2, way, d, t, j].astype(F32)
-                part[n, t, j] = total.astype(BF16)
-            return carry
-
-        lax.fori_loop(0, PER_CHIP, one, 0)
+            lax.fori_loop(0, PER_CHIP, add, 0)
         reduced(n).start()
         if n == 2:
             for rel in range(2):
                 gq_back(rel).start()
             for copy in gq_copies(0):
                 copy.start()
+        if n == 10 and dp_mates:
+            @pl.when(higher > 0)
+            def _():
+                pl.semaphore_wait(hello, higher)
         if n >= 2 and n % 4 == 2:
             sums.step()
+    for u in range(3):
+        def own_rest(j, carry, u=u):
+            for t in range(2):
+                rest[u, t, j] = own_terms(u, PER_CHIP * z + j, t)
+            return carry
+
+        lax.fori_loop(0, PER_CHIP, own_rest, 0)
     sums.finish()
 
     totals = gs_own[pl.ds(ctx, 1), :]
@@ -423,7 +463,7 @@
         if u < 3:
             def last(j, carry, u=u, ways=ways):
                 for t in range(2):
-                    total = own_terms(u, PER_CHIP * z + j, t)
+                    total = rest[u, t, j]
                     for way in ways:
                         total = total + inbox[u, way, 0, t, j].astype(F32)
                     fin[u, t, j] = total.astype(BF16)
@@ -488,6 +528,8 @@
         scratch_shapes=[
             kv, kv, kv, kv, rows, rows, rows,
             pltpu.VMEM((4, EMPTY + 1, 2, SLAB, HD), F32),
+            pltpu.VMEM((2, PER_CHIP, SLAB, HD), F32),
+            pltpu.VMEM((3, 2, PER_CHIP, SLAB, HD), F32),
             pltpu.VMEM((n_msgs, 2, PER_CHIP, SLAB, HD), BF16),
             pltpu.VMEM((4, 2, ARC, 2, PER_CHIP, SLAB, HD), BF16),
             pltpu.VMEM((2, PER_CHIP, WIN * SLAB, HD), F32),
@@ -501,6 +543,7 @@
             pltpu.SMEM((1, 2), F32),
             pltpu.SMEM((2 * EMPTY,), jnp.int32),
             pltpu.SMEM((2 * N_SLABS * PER_CHIP,), jnp.int32),
+            pltpu.SemaphoreType.REGULAR,
             dma((3,)), dma((3, 2)), dma((3, 2)), dma((3, 2)),
             dma((3, 2)), dma((3, 2)), dma((3, 2)), dma((2, 2)), dma((2, 2)),
             dma((4, 2, 2, 2)), dma((4, 2, 2, 2)),

time: 101 us -> 97 us (0.960)
  Pallas kernels: 97 us -> 93.4 us
    pallas_call x1, Pallas kernels: 97 us -> 93.4 us  [on_device(): pl.pallas_call(functools.partial(kernel, n_dp), out_shape=(jax.ShapeDtype...]
where the time goes in v4:
time: 97 us; the launch traced here: 96.9 us
  Pallas kernels  93.4 us (96%)
  local copies, waits for them, and re-layouts  2.89 us (3%)
    pallas_call x1, Pallas kernels, on_device(): pl.pallas_call(functools.partial(kernel, n_dp), out_shape=(jax.ShapeDtype...  93.4 us
    unnamed x4, local copies, waits for them, and re-layouts  2.89 us

profile of v4, /device:TPU:1, one launch (start us, length us, event | category | flops | bytes accessed | tf_op | source)
XLA Modules:
  0.0 96.9 jit_solution(16815046703390000739)
XLA Ops:
  0.6 93.4 %arc_attention.1 = (bf16[2,64,4096]{2,1,0:T(8,128)(2,1)S(1)}, bf16[2,64,1024]{2,1,0:T(8,128)(2,1)S(1)}, bf16[2,64,1024]{2,1,0:T(8,128)(2,1)S(1)}, f32[2]{0:T(128)S(1)}) custom-call(s32[1,32]{1,0:T(1,128)} %order_hbm.1, s32[1,16]{1,0:T(1,128)} %lens_hbm.1, f32[1,2]{1,0:T(1,128)} %bitcast.15, bf16[2,64,4096]{2,1,0:T(8,128)(2,1)} %bitcast.11, ...), custom_call_target="tpu_custom_call" | custom-call | tf_op jit(solution)/shard_map/arc_attention/pallas_call | solution.py:518
  94.0 1.0 %copy.15 = bf16[1,128,4096]{2,1,0:T(8,128)(2,1)} copy(bf16[1,128,4096]{2,1,0:T(8,128)(2,1)S(1)} %bitcast.8) | data formatting | bytes 2097152
  95.0 0.7 copy.16
  95.7 0.7 copy.17
  96.4 0.5 copy.18

commit v5 on v4

--- a/solution.py
+++ b/solution.py
@@ -25,6 +25,7 @@
 PER_CHIP = 4
 N_SLABS = N_Z * PER_CHIP
 EMPTY = PER_CHIP * WIN
+EARLY = 10
 
 SENDS = {(UP, 0): 2, (UP, 2): 4, (UP, 4): 6, (DOWN, 2): 5, (DOWN, 4): 3, (DOWN, 6): 1}
 GETS = {(UP, 0): 1, (UP, 2): 3, (UP, 4): 5, (DOWN, 0): 6, (DOWN, 2): 4, (DOWN, 4): 2}
@@ -50,7 +51,7 @@
            gq_out, gk_out, gv_out, gs_out,
            kv0, kv1, kv2, kv3, q_buf, g_buf, gq_buf, terms, ahead, rest, part, inbox, bias, fin,
            sink_own, sink_in, gs_own, gs_in, order, lens, sink, window, slot,
-           hello, small_sem, load_sem, swap_send, swap_recv, qg_load, qg_send, qg_recv, hand_send, hand_recv,
+           hello, far_hello, small_sem, load_sem, swap_send, swap_recv, qg_load, qg_send, qg_recv, hand_send, hand_recv,
            first_send, first_recv, ag_send, ag_recv, rs_send, rs_recv, gq_store, gq_send, gq_recv, back_send, back_recv,
            fin_store, fin_send, fin_recv, s_send, s_recv, t_send, t_recv):
     kvs = (kv0, kv1, kv2, kv3)
@@ -92,13 +93,15 @@
     for mates in dp_groups:
         for pick, mate in enumerate(mates, 1):
             dp_mates.append((mate, jnp.where(mate[0] > dp, 1, 0)))
+    far_mates = [(mate, jnp.where(mate[1] > ctx, 1, 0)) for mate in far_chips]
     higher = sum([above for _, above in dp_mates], jnp.int32(0))
+    far_higher = sum([above for _, above in far_mates], jnp.int32(0))
     barrier = pltpu.get_barrier_semaphore()
     greeted = [device(c, k) for c in (up_chip, down_chip) for k in (core, other)]
-    greeted += chip_pair[:1] + far_chips
+    greeted += chip_pair[:1]
     for mate in greeted:
         pl.semaphore_signal(barrier, inc=1, device_id=mate, device_id_type=MESH)
-    for mate, above in dp_mates:
+    for mate, above in far_mates + dp_mates:
         @pl.when(above == 1)
         def _(mate=mate):
             pl.semaphore_signal(barrier, inc=1, device_id=mate, device_id_type=MESH)
@@ -131,11 +134,8 @@
             loads.append(pltpu.make_async_copy(
                 qg_hbm[t].at[:, :, cols], qg_buf[t].at[u, own_rows], qg_load.at[u, t]))
 
-    pl.semaphore_wait(barrier, len(greeted) + len(dp_mates) - higher)
-    for mate, above in dp_mates:
-        @pl.when(above == 0)
-        def _(mate=mate):
-            pl.semaphore_signal(hello, inc=1, device_id=mate, device_id_type=MESH)
+    others = len(far_mates) + len(dp_mates) - far_higher - higher
+    pl.semaphore_wait(barrier, len(greeted) + others)
 
     def first(way, place, rel, t):
         of_core = (core, other)[rel]
@@ -150,6 +150,12 @@
         for rel in range(2):
             for t in range(2):
                 first(way, place, rel, t).start()
+
+    for back, mates in ((far_hello, far_mates), (hello, dp_mates)):
+        for mate, above in mates:
+            @pl.when(above == 0)
+            def _(mate=mate, back=back):
+                pl.semaphore_signal(back, inc=1, device_id=mate, device_id_type=MESH)
 
     for u in range(3):
         cols = columns(head_of(other, 2 * u), HD)
@@ -343,7 +349,11 @@
 
     sinks = Exchange(sink_own, sink_in, s_send, s_recv, [far_chips, chip_pair])
     for step in range(2, ARC + 1):
-        if step in (2, 4):
+        if step == 3:
+            @pl.when(far_higher > 0)
+            def _():
+                pl.semaphore_wait(far_hello, far_higher)
+        if step in (3, 4):
             sinks.step()
         for way, place in GATHER_ORDER:
             if step <= SENDS[way, place]:
@@ -395,6 +405,19 @@
         here = inbox.at[place // 2, way, d]
         return remote(here, here, rs_send.at[0], rs_recv.at[place // 2, way, d], (dp, peer))
 
+    def wait_sent():
+        for copy in swaps:
+            copy.wait_send()
+        for (way, place), count in SENDS.items():
+            for rel in range(2):
+                for t in range(2):
+                    first(way, place, rel, t).wait_send()
+            for step in range(2, count + 1):
+                gather(way, place, step).wait_send()
+        for rel in range(2):
+            for t in range(2):
+                hand(rel, t).wait_send()
+
     sums = Exchange(gs_own, gs_in, t_send, t_recv, [far_chips, chip_pair] + dp_groups)
     for n, (way, place, d) in enumerate(REDUCE_ORDER):
         owner = chip(d if way == UP else -d)
@@ -424,12 +447,16 @@
                 gq_back(rel).start()
             for copy in gq_copies(0):
                 copy.start()
+        if n == 12:
+            wait_sent()
         if n == 10 and dp_mates:
             @pl.when(higher > 0)
             def _():
                 pl.semaphore_wait(hello, higher)
         if n >= 2 and n % 4 == 2:
             sums.step()
+    for n in range(EARLY):
+        reduced(n).wait_send()
     for u in range(3):
         def own_rest(j, carry, u=u):
             for t in range(2):
@@ -456,7 +483,7 @@
         there = gkv_out[t].at[:, :, columns(head_of(other, 2 * u), HD)]
         return remote(there, there, fin_send.at[u, t], fin_recv.at[u, t], (dp, peer))
 
-    for place, ways in ((6, (UP,)), (0, (DOWN,)), (2, (UP, DOWN)), (4, (UP, DOWN))):
+    for place, ways in ((2, (UP, DOWN)), (4, (DOWN, UP)), (0, (DOWN,)), (6, (UP,))):
         u = place // 2
         for way in ways:
             came_in(way, place, 0).wait_recv()
@@ -474,19 +501,9 @@
             for copy in fin_copies(u, t):
                 copy.start()
 
-    for copy in swaps:
-        copy.wait_send()
-    for (way, place), count in SENDS.items():
-        for rel in range(2):
-            for t in range(2):
-                first(way, place, rel, t).wait_send()
-        for step in range(2, count + 1):
-            gather(way, place, step).wait_send()
-    for n in range(len(REDUCE_ORDER)):
+    for n in range(EARLY, len(REDUCE_ORDER)):
         reduced(n).wait_send()
     for rel in range(2):
-        for t in range(2):
-            hand(rel, t).wait_send()
         gq_back(rel).wait_send()
         gq_returned(rel).wait_recv()
     for u in range(3):
@@ -494,7 +511,7 @@
         keep.wait()
         away.wait_send()
         gq_arrived(u).wait_recv()
-    for u in (3, 0, 1, 2):
+    for u in (1, 2, 0, 3):
         for t in range(2):
             keep, away = fin_copies(u, t)
             keep.wait()
@@ -543,7 +560,7 @@
             pltpu.SMEM((1, 2), F32),
             pltpu.SMEM((2 * EMPTY,), jnp.int32),
             pltpu.SMEM((2 * N_SLABS * PER_CHIP,), jnp.int32),
-            pltpu.SemaphoreType.REGULAR,
+            pltpu.SemaphoreType.REGULAR, pltpu.SemaphoreType.REGULAR,
             dma((3,)), dma((3, 2)), dma((3, 2)), dma((3, 2)),
             dma((3, 2)), dma((3, 2)), dma((3, 2)), dma((2, 2)), dma((2, 2)),
             dma((4, 2, 2, 2)), dma((4, 2, 2, 2)),

time: 97 us -> 96.1 us (level)
  no operation moved by 1% of the time
where the time goes in v5:
time: 96.1 us; the launch traced here: 96 us
  Pallas kernels  92.5 us (96%)
  local copies, waits for them, and re-layouts  2.89 us (3%)
    pallas_call x1, Pallas kernels, on_device(): pl.pallas_call(functools.partial(kernel, n_dp), out_shape=(jax.ShapeDtype...  92.5 us
    unnamed x4, local copies, waits for them, and re-layouts  2.89 us

profile of v5, /device:TPU:1, one launch (start us, length us, event | category | flops | bytes accessed | tf_op | source)
XLA Modules:
  0.0 96.0 jit_solution(2743572119066901381)
XLA Ops:
  0.6 92.5 %arc_attention.1 = (bf16[2,64,4096]{2,1,0:T(8,128)(2,1)S(1)}, bf16[2,64,1024]{2,1,0:T(8,128)(2,1)S(1)}, bf16[2,64,1024]{2,1,0:T(8,128)(2,1)S(1)}, f32[2]{0:T(128)S(1)}) custom-call(s32[1,32]{1,0:T(1,128)} %order_hbm.1, s32[1,16]{1,0:T(1,128)} %lens_hbm.1, f32[1,2]{1,0:T(1,128)} %bitcast.15, bf16[2,64,4096]{2,1,0:T(8,128)(2,1)} %bitcast.11, ...), custom_call_target="tpu_custom_call" | custom-call | tf_op jit(solution)/shard_map/arc_attention/pallas_call | solution.py:535
  93.1 1.0 %copy.15 = bf16[1,128,4096]{2,1,0:T(8,128)(2,1)} copy(bf16[1,128,4096]{2,1,0:T(8,128)(2,1)S(1)} %bitcast.8) | data formatting | bytes 2097152
  94.1 0.7 copy.16
  94.8 0.7 copy.17
  95.5 0.5 copy.18
